TPU v7x, 128 devices: a whole 4x4x4 slice. The times are simulated.
128 devices in a mesh: dp: 32 (over z, x, core), mp: 4 (over y).
Axes of the slice: x: 4, y: 4, z: 4, core: 2. Of those that a mesh axis runs over, the one named last changes fastest.
Arguments:
- candidates: int32 [512, 3], P('dp'), may hold values from 0 to 31, as said below
- row_lengths: int32 [512, 2], P('dp'), may hold values from 1 to 128
- enc_bank: bfloat16 [512, 128, 2048], P('dp', None, 'mp'), may hold values from -480 to 480
- dec_bank: bfloat16 [512, 128, 2048], P('dp', None, 'mp'), may hold values from -6 to 6
- w_query: bfloat16 [2048, 2048], P(None, 'mp'), may hold values from -0.125 to 0.125
- w_key: bfloat16 [2048, 2048], P(None, 'mp'), may hold values from -0.125 to 0.125
- w_value: bfloat16 [2048, 2048], P(None, 'mp'), may hold values from -0.125 to 0.125
Outputs:
- contexts: bfloat16 [768, 128, 2048], P('dp', None, 'mp')
Inputs may be any that keep to these rules, and one draw needn't show every extreme that they name: `candidates`: row ids in columns 0 and 1 index the same shard's banks (0 to 15), column 2 is a group (0 to 31). A shard sends either none or exactly 2 pairs to a group; a group receives at most 24 pairs in all, and some group exactly 24.
All inputs are finite; a program needn't handle non-finite values.
Results may differ from a plain program's by a relative error of at most 0.0045.
The roundings to bfloat16 on the way count: a program that leaves them out, or rounds other values in their place, can miss the bound.
Values may be sent and summed in bfloat16 or wider, within the bound.
No kernel may reach another device: no remote copies, remote signals or barrier semaphores. Data moves between devices by JAX's collectives and lax.ppermute only.
A program may use at most 128 MiB of HBM per device.

v0:
```python
import functools
import math

import jax
import jax.numpy as jnp
from jax import lax
from jax.experimental import pallas as pl
from jax.experimental.pallas import tpu as pltpu
from jax.sharding import PartitionSpec as P

D = 2048
HD = 128
L = 128
GCAP = 24
BLOCK = 16
BLOCKS = L // BLOCK
TILE = 256
SIZES = (1408, 1536, 1664, 1792, 1920, 2048, 2304, 4096)
VMEM = pl.BlockSpec(memory_space=pltpu.VMEM)
SMEM = pl.BlockSpec(memory_space=pltpu.SMEM)
HBM = pl.BlockSpec(memory_space=pltpu.HBM)


def pack_kernel(cand, lens, enc, dec, out_pairs, facts, out, staged, starts, arrived):
    rows = enc.shape[0] // L
    count = cand.shape[1]
    for row in range(rows):
        starts[0, row] = 0
        starts[1, row] = 0
    for c in range(count):
        starts[0, cand[0, c]] = 1
        starts[1, cand[1, c]] = 1
    banks = (enc, dec)

    def load(column, row):
        at = slice(row * L, (row + 1) * L)
        return pltpu.make_async_copy(banks[column].at[at], staged.at[column, at], arrived.at[column, row])

    for column in range(2):
        for row in range(rows):

            @pl.when(starts[column, row] > 0)
            def _(column=column, row=row):
                load(column, row).start()

    total = jnp.int32(0)
    for column in range(2):
        for row in range(rows):
            needed = starts[column, row] > 0
            blocks = jnp.where(needed, (lens[column, row] + BLOCK - 1) // BLOCK, 0)
            starts[column, row] = total * BLOCK

            @pl.when(needed)
            def _(column=column, row=row):
                load(column, row).wait()

            def move(b, carry, column=column, row=row, first=total):
                to = pl.multiple_of((first + b) * BLOCK, BLOCK)
                out[pl.ds(to, BLOCK), :] = staged[column, pl.ds(pl.multiple_of(row * L + b * BLOCK, BLOCK), BLOCK), :]
                return carry

            lax.fori_loop(0, blocks, move, 0)
            total = total + blocks
        facts[1 + column] = total * BLOCK
    bucket = jnp.int32(0)
    size = jnp.int32(SIZES[0])
    for low, high in zip(SIZES, SIZES[1:]):
        over = total * BLOCK > low
        bucket = bucket + over.astype(jnp.int32)
        size = jnp.where(over, high, size)
    facts[0] = bucket

    def place(c, carry):
        s, t = cand[0, c], cand[1, c]
        out_pairs[0, c] = starts[0, s]
        out_pairs[1, c] = starts[1, t]
        out_pairs[2, c] = lens[0, s]
        out_pairs[3, c] = lens[1, t]
        out_pairs[4, c] = cand[2, c]
        return carry

    lax.fori_loop(0, count, place, 0)

    def clear(b, carry):
        out[pl.ds(pl.multiple_of(b * BLOCK, BLOCK), BLOCK), :] = jnp.zeros((BLOCK, out.shape[1]), out.dtype)
        return carry

    lax.fori_loop(total, size // BLOCK, clear, 0)


def assemble_kernel(*refs):
    pieces, (out1, out2, out3, done) = refs[:8], refs[8:]
    half = pieces[0].shape[0]
    quarter = half // 2
    outs = (out1.at[:half], out3.at[:half], out1.at[half : 2 * half], out3.at[half : 2 * half]) + tuple(
        out2.at[k * quarter : (k + 1) * quarter] for k in range(4)
    )
    copies = [pltpu.make_async_copy(piece, out, done.at[k]) for k, (piece, out) in enumerate(zip(pieces, outs))]
    for copy in copies:
        copy.start()
    for copy in copies:
        copy.wait()


def attend_kernel(facts, pairs, x0, x1, x2, x3, wq, wk, wv, out, xs, keys, values, queries, turned, arrived):
    width = x0.shape[1]
    heads = width // HD
    me = lax.axis_index("mp")
    origin = [pl.multiple_of(lax.rem(me + (4 - d), 4) * width, width) for d in range(4)]
    source = pl.multiple_of(facts[1], BLOCK)
    target = facts[2] - facts[1]
    count = pairs.shape[1]
    chunks = (facts[2] + TILE - 1) // TILE
    tiles = (source + TILE - 1) // TILE

    def loads(i):
        rows = pl.ds(pl.multiple_of(i * TILE, TILE), TILE)
        return [
            pltpu.make_async_copy(x.at[rows], xs.at[d, rows], arrived.at[d, i]) for d, x in enumerate((x0, x1, x2, x3))
        ]

    def begin(i, carry):
        for copy in loads(i):
            copy.start()
        return carry

    def finish(i, carry):
        for copy in loads(i):
            copy.wait()
        return carry

    lax.fori_loop(0, chunks, begin, 0)

    def kv_tile(i, carry):
        finish(i, 0)
        rows = pl.ds(pl.multiple_of(i * TILE, TILE), TILE)
        key_sum = jnp.zeros((TILE, width), jnp.float32)
        value_sum = jnp.zeros((TILE, width), jnp.float32)
        for d in range(4):
            x = xs[d, rows, :]
            key_sum += jnp.dot(x, wk[pl.ds(origin[d], width), :], preferred_element_type=jnp.float32)
            value_sum += jnp.dot(x, wv[pl.ds(origin[d], width), :], preferred_element_type=jnp.float32)
        keys[rows, :] = key_sum.astype(jnp.bfloat16)
        values[rows, :] = value_sum.astype(jnp.bfloat16)
        return carry

    lax.fori_loop(0, tiles, kv_tile, 0)
    values[pl.ds(source, L), :] = jnp.zeros((L, width), jnp.bfloat16)
    lax.fori_loop(tiles, chunks, finish, 0)

    def q_tile(i, carry):
        rows = pl.ds(pl.multiple_of(source + i * TILE, BLOCK), TILE)
        parts = [xs[d, rows, :].astype(jnp.float32) for d in range(4)]
        mean = sum(jnp.sum(x, axis=-1, keepdims=True) for x in parts) * (1.0 / D)
        parts = [x - mean for x in parts]
        variance = sum(jnp.sum(x * x, axis=-1, keepdims=True) for x in parts) * (1.0 / D)
        scale = lax.rsqrt(variance + 1e-05)
        total = jnp.zeros((TILE, width), jnp.float32)
        for x, start in zip(parts, origin):
            total += jnp.dot(
                (x * scale).astype(jnp.bfloat16), wq[pl.ds(start, width), :], preferred_element_type=jnp.float32
            )
        queries[pl.ds(pl.multiple_of(i * TILE, TILE), TILE), :] = total.astype(jnp.bfloat16)
        return carry

    lax.fori_loop(0, (target + TILE - 1) // TILE, q_tile, 0)
    column = lax.broadcasted_iota(jnp.int32, (L, L), 1)
    line = lax.broadcasted_iota(jnp.int32, (L, HD), 0)

    def pair(p, carry):
        s_at = pl.multiple_of(pairs[0, p], BLOCK)
        t_at = pl.multiple_of(pairs[1, p] - source, BLOCK)
        key_mask = column < pairs[2, p]
        query_mask = line < pairs[3, p]
        cols = [slice(h * HD, (h + 1) * HD) for h in range(heads)]
        scores = [
            lax.dot_general(
                queries[pl.ds(t_at, L), c],
                keys[pl.ds(s_at, L), c],
                (((1,), (1,)), ((), ())),
                preferred_element_type=jnp.float32,
            )
            for c in cols
        ]
        scores = [jnp.where(key_mask, s * (1.0 / math.sqrt(HD)), -1e30) for s in scores]
        tops = [jnp.max(s, axis=-1, keepdims=True) for s in scores]
        terms = [jnp.exp(s - top) for s, top in zip(scores, tops)]
        sums = [jnp.sum(t, axis=-1, keepdims=True) for t in terms]
        weights = [(t * (1.0 / total)).astype(jnp.bfloat16) for t, total in zip(terms, sums)]
        contexts = [
            jnp.dot(w, values[pl.ds(s_at, L), c], preferred_element_type=jnp.float32)
            for w, c in zip(weights, cols)
        ]
        for h, context in enumerate(contexts):
            context = jnp.where(query_mask, context, 0.0)
            for g in range(4):
                turned[h + g * heads, pl.ds(p, 32, stride=count), :] = context[g * 32 : (g + 1) * 32]
        return carry

    lax.fori_loop(0, count, pair, 0)
    for k in range(4 * heads):
        g, h = k // heads, k % heads
        at = g * width + h * HD
        out[:, at : at + HD] = turned[k].astype(jnp.bfloat16)
    line = lax.broadcasted_iota(jnp.int32, (count, HD), 0)
    groups = jnp.zeros((count, HD), jnp.float32)
    for p in range(count):
        groups = jnp.where(line == p, pairs[4, p].astype(jnp.float32), groups)
    for j in range(32):
        out[j * count : (j + 1) * count, 4 * width :] = groups.astype(jnp.bfloat16)


def route_kernel(x, out):
    total = x.shape[0]
    width = out.shape[1]
    mine = x[:, width : width + 1].astype(jnp.float32)
    a = lax.broadcasted_iota(jnp.int32, (total, total), 0)
    b = lax.broadcasted_iota(jnp.int32, (total, total), 1)
    ones = jnp.ones((16, total), jnp.bfloat16)
    spread = jnp.where(a == b, mine, 0.0).astype(jnp.bfloat16)
    group = jnp.dot(ones, spread, preferred_element_type=jnp.float32)[:1]
    before = jnp.where((mine == group) & (a < b), 1.0, 0.0).astype(jnp.bfloat16)
    rank = jnp.dot(ones, before, preferred_element_type=jnp.float32)[:1]
    slot = (group * GCAP + rank).astype(jnp.int32)
    choose = lax.broadcasted_iota(jnp.int32, (out.shape[0], total), 0) == slot
    choose = jnp.where(choose, 1.0, 0.0).astype(jnp.bfloat16)
    for c in range(0, width, 256):
        out[:, c : c + 256] = jnp.dot(choose, x[:, c : c + 256], preferred_element_type=jnp.float32).astype(
            jnp.bfloat16
        )


def place_kernel(x, out, wide):
    slots, pieces, width = out.shape
    for c in range(width // HD):
        cols = slice(c * HD, (c + 1) * HD)
        wide[c] = x[:, cols].astype(jnp.float32)
    for q in range(slots):
        for c in range(width // HD):
            out[q, :, c * HD : (c + 1) * HD] = wide[c, pl.ds(q, pieces, stride=slots), :].astype(jnp.bfloat16)


def gather(size, packed):
    half, quarter = size // 2, size // 4
    send = lambda x, step: lax.ppermute(x, "mp", [(i, (i + step) % 4) for i in range(4)])
    direct, across = [], []
    for c in range(2):
        own = packed[c * half : (c + 1) * half]
        direct += [send(own, 1), send(own, 3)]
    for c in range(2):
        across += [send(direct[2 * c][:quarter], 1), send(direct[2 * c + 1][quarter:], 3)]
    return pl.pallas_call(
        assemble_kernel,
        out_shape=[jax.ShapeDtypeStruct(packed.shape, jnp.bfloat16)] * 3,
        in_specs=[VMEM] * 8,
        out_specs=[HBM] * 3,
        scratch_shapes=[pltpu.SemaphoreType.DMA((8,))],
        compiler_params=pltpu.CompilerParams(vmem_limit_bytes=13 * 2**20),
    )(*direct, *across)


def attend(facts, pairs, x0, x1, x2, x3, wq, wk, wv):
    total, width = x0.shape
    rows = total // 2
    n = pairs.shape[1] * 32
    return pl.pallas_call(
        attend_kernel,
        out_shape=jax.ShapeDtypeStruct((n, 4 * width + HD), jnp.bfloat16),
        in_specs=[SMEM, SMEM, VMEM] + [HBM] * 3 + [VMEM] * 3,
        out_specs=VMEM,
        scratch_shapes=[
            pltpu.VMEM((4, total + TILE, width), jnp.bfloat16),
            pltpu.VMEM((rows + L, width), jnp.bfloat16),
            pltpu.VMEM((rows + L, width), jnp.bfloat16),
            pltpu.VMEM((rows + L, width), jnp.bfloat16),
            pltpu.VMEM((4 * width // HD, n, HD), jnp.float32),
            pltpu.SemaphoreType.DMA((4, total // TILE)),
        ],
        compiler_params=pltpu.CompilerParams(vmem_limit_bytes=50 * 2**20),
    )(facts, pairs, x0, x1, x2, x3, wq, wk, wv)


def on_device(candidates, row_lengths, enc_bank, dec_bank, w_query, w_key, w_value):
    shards = lax.axis_size("dp")
    count = candidates.shape[0]
    bank = enc_bank.shape[0]
    width = enc_bank.shape[2]
    rows = bank * L
    pairs, facts, packed = pl.pallas_call(
        pack_kernel,
        out_shape=[
            jax.ShapeDtypeStruct((5, count), jnp.int32),
            jax.ShapeDtypeStruct((3,), jnp.int32),
            jax.ShapeDtypeStruct((2 * rows, width), jnp.bfloat16),
        ],
        in_specs=[SMEM, SMEM, HBM, HBM],
        out_specs=[SMEM, SMEM, VMEM],
        scratch_shapes=[
            pltpu.VMEM((2, rows, width), jnp.bfloat16),
            pltpu.SMEM((2, bank), jnp.int32),
            pltpu.SemaphoreType.DMA((2, bank)),
        ],
        compiler_params=pltpu.CompilerParams(vmem_limit_bytes=58 * 2**20),
    )(candidates.T, row_lengths.T, enc_bank.reshape(rows, width), dec_bank.reshape(rows, width))
    x1, x2, x3 = lax.switch(facts[0], [functools.partial(gather, size) for size in SIZES], packed)
    context = attend(facts, pairs, packed, x1, x2, x3, w_query, w_key, w_value)
    spread = lax.all_to_all(context.reshape(shards, count, 4 * width + HD), "dp", 0, 0, tiled=True)
    routed = pl.pallas_call(
        route_kernel,
        out_shape=jax.ShapeDtypeStruct((shards * GCAP, 4 * width), jnp.bfloat16),
        in_specs=[VMEM],
        out_specs=VMEM,
        compiler_params=pltpu.CompilerParams(vmem_limit_bytes=40 * 2**20),
    )(spread.reshape(shards * count, 4 * width + HD))
    arrived = lax.all_to_all(routed.reshape(shards, GCAP, 4 * width), "dp", 0, 0, tiled=True)
    return pl.pallas_call(
        place_kernel,
        grid=(4,),
        out_shape=jax.ShapeDtypeStruct((GCAP, L, width), jnp.bfloat16),
        in_specs=[pl.BlockSpec((shards * GCAP, width), lambda g: (0, g))],
        out_specs=pl.BlockSpec((GCAP, 32, width), lambda g: (0, g, 0)),
        scratch_shapes=[pltpu.VMEM((width // HD, shards * GCAP, HD), jnp.float32)],
        compiler_params=pltpu.CompilerParams(vmem_limit_bytes=40 * 2**20),
    )(arrived.reshape(shards * GCAP, 4 * width))


def solution(mesh):
    placed = (
        P("dp", None),
        P("dp", None),
        P("dp", None, "mp"),
        P("dp", None, "mp"),
        P(None, "mp"),
        P(None, "mp"),
        P(None, "mp"),
    )
    return jax.shard_map(on_device, mesh=mesh, in_specs=placed, out_specs=P("dp", None, "mp"), check_vma=False)
```

profile of v0, /device:TPU:1, one launch (start us, length us, event | category | flops | bytes accessed | tf_op | source)
XLA Modules:
  0.0 191.0 jit_solution(6672250358796841167)
XLA Ops:
  0.0 5.2 %shard_map.73 = (s32[5,16]{1,0:T(8,128)}, s32[3]{0:T(128)}, bf16[4096,512]{1,0:T(8,128)(2,1)}) custom-call(s32[3,16]{1,0:T(4,128)} %bitcast.17, s32[2,16]{1,0:T(2,128)} %bitcast.18, bf16[2048,512]{1,0:T(8,128)(2,1)} %bitcast.15, bf16[2048,512]{1,0:T(8,128)(2,1)} %bitcast.16), custom_call_target="tpu_custom_call" | custom-call | tf_op jit(solution)/shard_map/pallas_call | solution.py:289
  6.0 0.0 copy-start
  6.0 0.0 copy-start.1
  6.0 0.0 copy-start.2
  6.0 56.5 %conditional.1 = ((bf16[4096,512]{1,0:T(8,128)(2,1)}, bf16[4096,512]{1,0:T(8,128)(2,1)}, bf16[4096,512]{1,0:T(8,128)(2,1)})) conditional(s32[]{:T(128)} %bitcast.4, bf16[4096,512]{1,0:T(8,128)(2,1)} %get-tuple-element.21.x0, bf16[4096,512]{1,0:T(8,128)(2,1)} %get-tuple-element.21.x0, ...), branch_computations={%region_0.0_spmd, %region_1.0_spmd, %region_2.0_spmd, %region_3.0_... | conditional | bytes 67109192 | solution.py:305
  6.0 1.6 fusion
  7.6 3.6 %collective-permute-start.3 = (bf16[704,512]{1,0:T(8,128)(2,1)S(1)}, bf16[704,512]{1,0:T(8,128)(2,1)S(1)}, u32[]{:S(2)}, u32[]{:S(2)}) collective-permute-start(bf16[704,512]{1,0:T(8,128)(2,1)S(1)} %get-tuple-element.25), channel_id=1, source_target_pairs={{0,3},{1,0},{2,1},{3,2},{4,7},{5,4},{6,5},{7,6},{8,11},{9,8},{10,9... | collective-permute-start | bytes 2162696 | tf_op jit(solution)/shard_map/cond/branch_0_fun/ppermute | solution.py:245
  11.2 0.0 collective-permute-start.2
  11.2 2.7 %collective-permute-start.1 = (bf16[704,512]{1,0:T(8,128)(2,1)S(1)}, bf16[704,512]{1,0:T(8,128)(2,1)S(1)}, u32[]{:S(2)}, u32[]{:S(2)}) collective-permute-start(bf16[704,512]{1,0:T(8,128)(2,1)S(1)} %get-tuple-element.26), channel_id=1, source_target_pairs={{0,3},{1,0},{2,1},{3,2},{4,7},{5,4},{6,5},{7,6},{8,11},{9,8},{10,9... | collective-permute-start | bytes 2162696 | tf_op jit(solution)/shard_map/cond/branch_0_fun/ppermute | solution.py:245
  13.9 0.0 collective-permute-start
  13.9 12.1 %collective-permute-done.3.refs_3_ = bf16[704,512]{1,0:T(8,128)(2,1)S(1)} collective-permute-done((bf16[704,512]{1,0:T(8,128)(2,1)S(1)}, bf16[704,512]{1,0:T(8,128)(2,1)S(1)}, u32[]{:S(2)}, u32[]{:S(2)}) %collective-permute-start.3) | collective-permute-done | bytes 720928 | tf_op jit(solution)/shard_map/cond/branch_0_fun/ppermute | solution.py:245
  26.0 3.5 %collective-permute-start.7 = (bf16[352,512]{1,0:T(8,128)(2,1)S(1)}, bf16[352,512]{1,0:T(8,128)(2,1)S(1)}, u32[]{:S(2)}, u32[]{:S(2)}) collective-permute-start(bf16[352,512]{1,0:T(8,128)(2,1)S(1)} %slice.151), channel_id=1, source_target_pairs={{0,3},{1,0},{2,1},{3,2},{4,7},{5,4},{6,5},{7,6},{8,11},{9,8},{10,9... | collective-permute-start | bytes 1081352 | tf_op jit(solution)/shard_map/cond/branch_0_fun/ppermute | solution.py:245
  29.5 0.0 collective-permute-done.2.refs_2_
  29.5 0.1 collective-permute-start.6
  29.6 11.8 %collective-permute-done.1.refs_1_ = bf16[704,512]{1,0:T(8,128)(2,1)S(1)} collective-permute-done((bf16[704,512]{1,0:T(8,128)(2,1)S(1)}, bf16[704,512]{1,0:T(8,128)(2,1)S(1)}, u32[]{:S(2)}, u32[]{:S(2)}) %collective-permute-start.1) | collective-permute-done | bytes 720928 | tf_op jit(solution)/shard_map/cond/branch_0_fun/ppermute | solution.py:245
  41.4 3.5 %collective-permute-start.5 = (bf16[352,512]{1,0:T(8,128)(2,1)S(1)}, bf16[352,512]{1,0:T(8,128)(2,1)S(1)}, u32[]{:S(2)}, u32[]{:S(2)}) collective-permute-start(bf16[352,512]{1,0:T(8,128)(2,1)S(1)} %slice.149), channel_id=1, source_target_pairs={{0,3},{1,0},{2,1},{3,2},{4,7},{5,4},{6,5},{7,6},{8,11},{9,8},{10,9... | collective-permute-start | bytes 1081352 | tf_op jit(solution)/shard_map/cond/branch_0_fun/ppermute | solution.py:245
  44.9 0.0 collective-permute-done.refs_0_
  45.0 0.1 collective-permute-start.4
  45.0 4.1 %collective-permute-done.7.refs_7_ = bf16[352,512]{1,0:T(8,128)(2,1)S(1)} collective-permute-done((bf16[352,512]{1,0:T(8,128)(2,1)S(1)}, bf16[352,512]{1,0:T(8,128)(2,1)S(1)}, u32[]{:S(2)}, u32[]{:S(2)}) %collective-permute-start.7) | collective-permute-done | bytes 360480 | tf_op jit(solution)/shard_map/cond/branch_0_fun/ppermute | solution.py:245
  49.1 3.1 %collective-permute-done.6.refs_6_ = bf16[352,512]{1,0:T(8,128)(2,1)S(1)} collective-permute-done((bf16[352,512]{1,0:T(8,128)(2,1)S(1)}, bf16[352,512]{1,0:T(8,128)(2,1)S(1)}, u32[]{:S(2)}, u32[]{:S(2)}) %collective-permute-start.6) | collective-permute-done | bytes 360480 | tf_op jit(solution)/shard_map/cond/branch_0_fun/ppermute | solution.py:245
  52.2 4.6 %collective-permute-done.5.refs_5_ = bf16[352,512]{1,0:T(8,128)(2,1)S(1)} collective-permute-done((bf16[352,512]{1,0:T(8,128)(2,1)S(1)}, bf16[352,512]{1,0:T(8,128)(2,1)S(1)}, u32[]{:S(2)}, u32[]{:S(2)}) %collective-permute-start.5) | collective-permute-done | bytes 360480 | tf_op jit(solution)/shard_map/cond/branch_0_fun/ppermute | solution.py:245
  56.9 3.1 %collective-permute-done.4.refs_4_ = bf16[352,512]{1,0:T(8,128)(2,1)S(1)} collective-permute-done((bf16[352,512]{1,0:T(8,128)(2,1)S(1)}, bf16[352,512]{1,0:T(8,128)(2,1)S(1)}, u32[]{:S(2)}, u32[]{:S(2)}) %collective-permute-start.4) | collective-permute-done | bytes 360480 | tf_op jit(solution)/shard_map/cond/branch_0_fun/ppermute | solution.py:245
  60.0 2.1 %branch_0_fun.1 = (bf16[4096,512]{1,0:T(8,128)(2,1)}, bf16[4096,512]{1,0:T(8,128)(2,1)}, bf16[4096,512]{1,0:T(8,128)(2,1)}) custom-call(bf16[704,512]{1,0:T(8,128)(2,1)S(1)} %collective-permute-done.refs_0_, bf16[704,512]{1,0:T(8,128)(2,1)S(1)} %collective-permute-done.1.refs_1_, bf16[704,512]{1,0:T(8,128)(2,1)S(1)} %collective-permute-done.2.refs_2_, ...), custom_call_target="tpu_custom_call" | custom-call | tf_op jit(solution)/shard_map/cond/branch_0_fun/pallas_call | solution.py:252
  62.4 0.0 copy-done
  62.5 0.0 copy-done.1
  62.5 0.0 copy-done.2
  62.5 23.3 %shard_map.74 = bf16[512,2176]{1,0:T(8,128)(2,1)} custom-call(s32[3]{0:T(128)S(1)} %copy-done.2, s32[5,16]{1,0:T(8,128)S(1)} %copy-done.1, bf16[4096,512]{1,0:T(8,128)(2,1)} %get-tuple-element.21.x0, bf16[4096,512]{1,0:T(8,128)(2,1)} %get-tuple-element.22.x1, bf16[4096,512]{1,0:T(8,128)(2,1)} %get-tuple-element.23.x2, ...), custom_call_target="tpu_custom_call" | custom-call | tf_op jit(solution)/shard_map/pallas_call | solution.py:266
  85.8 56.6 %all_to_all.10 = bf16[32,16,2176]{2,1,0:T(8,128)(2,1)S(1)} all-to-all(bf16[32,16,2176]{2,1,0:T(8,128)(2,1)} %bitcast.14), channel_id=1, replica_groups=mesh['dp'=32,'mp'=4] {'dp'}, dimensions={0} | all-to-all | bytes 4456448 | tf_op jit(solution)/shard_map/all_to_all | solution.py:307
  142.4 2.2 %shard_map.75 = bf16[768,2048]{1,0:T(8,128)(2,1)S(1)} custom-call(bf16[512,2176]{1,0:T(8,128)(2,1)S(1)} %bitcast.12), custom_call_target="tpu_custom_call" | custom-call | tf_op jit(solution)/shard_map/pallas_call | solution.py:308
  144.6 43.2 %all_to_all.11 = bf16[32,24,2048]{2,1,0:T(8,128)(2,1)S(1)} all-to-all(bf16[32,24,2048]{2,1,0:T(8,128)(2,1)S(1)} %bitcast.11), channel_id=1, replica_groups=mesh['dp'=32,'mp'=4] {'dp'}, dimensions={0} | all-to-all | bytes 6291456 | tf_op jit(solution)/shard_map/all_to_all | solution.py:315
  187.8 3.2 %shard_map.76 = bf16[24,128,512]{2,1,0:T(8,128)(2,1)} custom-call(bf16[768,2048]{1,0:T(8,128)(2,1)S(1)} %bitcast.10), custom_call_target="tpu_custom_call" | custom-call | tf_op jit(solution)/shard_map/pallas_call | solution.py:316
  (4 shorter events, 0.1 us)
Async XLA Ops:
  6.0 56.5 %copy-start = (bf16[2048,512]{1,0:T(8,128)(2,1)S(1)}, bf16[2048,512]{1,0:T(8,128)(2,1)}, u32[]{:S(2)}) copy-start(bf16[2048,512]{1,0:T(8,128)(2,1)} %wq.1) | copy-start | bytes 6291460
  6.0 56.5 %copy-start.1 = (s32[5,16]{1,0:T(8,128)S(1)}, s32[5,16]{1,0:T(8,128)}, u32[]{:S(2)}) copy-start(s32[5,16]{1,0:T(8,128)} %get-tuple-element.20.pairs) | copy-start | bytes 964
  6.0 56.5 %copy-start.2 = (s32[3]{0:T(128)S(1)}, s32[3]{0:T(128)}, u32[]{:S(2)}) copy-start(s32[3]{0:T(128)} %get-tuple-element.19.facts) | copy-start | bytes 40
  7.6 18.4 %collective-permute-start.3 = (bf16[704,512]{1,0:T(8,128)(2,1)S(1)}, bf16[704,512]{1,0:T(8,128)(2,1)S(1)}, u32[]{:S(2)}, u32[]{:S(2)}) collective-permute-start(bf16[704,512]{1,0:T(8,128)(2,1)S(1)} %get-tuple-element.25), channel_id=1, source_target_pairs={{0,3},{1,0},{2,1},{3,2},{4,7},{5,4},{6,5},{7,6},{8,11},{9,8},{10,9... | collective-permute-start | bytes 2162696 | tf_op jit(solution)/shard_map/cond/branch_0_fun/ppermute | solution.py:245
  11.2 18.3 %collective-permute-start.2 = (bf16[704,512]{1,0:T(8,128)(2,1)S(1)}, bf16[704,512]{1,0:T(8,128)(2,1)S(1)}, u32[]{:S(2)}, u32[]{:S(2)}) collective-permute-start(bf16[704,512]{1,0:T(8,128)(2,1)S(1)} %get-tuple-element.25), channel_id=1, source_target_pairs={{0,1},{1,2},{2,3},{3,0},{4,5},{5,6},{6,7},{7,4},{8,9},{9,10},{10,1... | collective-permute-start | bytes 2162696 | tf_op jit(solution)/shard_map/cond/branch_0_fun/ppermute | solution.py:245
  11.2 30.2 %collective-permute-start.1 = (bf16[704,512]{1,0:T(8,128)(2,1)S(1)}, bf16[704,512]{1,0:T(8,128)(2,1)S(1)}, u32[]{:S(2)}, u32[]{:S(2)}) collective-permute-start(bf16[704,512]{1,0:T(8,128)(2,1)S(1)} %get-tuple-element.26), channel_id=1, source_target_pairs={{0,3},{1,0},{2,1},{3,2},{4,7},{5,4},{6,5},{7,6},{8,11},{9,8},{10,9... | collective-permute-start | bytes 2162696 | tf_op jit(solution)/shard_map/cond/branch_0_fun/ppermute | solution.py:245
  13.9 31.0 %collective-permute-start = (bf16[704,512]{1,0:T(8,128)(2,1)S(1)}, bf16[704,512]{1,0:T(8,128)(2,1)S(1)}, u32[]{:S(2)}, u32[]{:S(2)}) collective-permute-start(bf16[704,512]{1,0:T(8,128)(2,1)S(1)} %get-tuple-element.26), channel_id=1, source_target_pairs={{0,1},{1,2},{2,3},{3,0},{4,5},{5,6},{6,7},{7,4},{8,9},{9,10},{10,1... | collective-permute-start | bytes 2162696 | tf_op jit(solution)/shard_map/cond/branch_0_fun/ppermute | solution.py:245
  26.0 23.1 %collective-permute-start.7 = (bf16[352,512]{1,0:T(8,128)(2,1)S(1)}, bf16[352,512]{1,0:T(8,128)(2,1)S(1)}, u32[]{:S(2)}, u32[]{:S(2)}) collective-permute-start(bf16[352,512]{1,0:T(8,128)(2,1)S(1)} %slice.151), channel_id=1, source_target_pairs={{0,3},{1,0},{2,1},{3,2},{4,7},{5,4},{6,5},{7,6},{8,11},{9,8},{10,9... | collective-permute-start | bytes 1081352 | tf_op jit(solution)/shard_map/cond/branch_0_fun/ppermute | solution.py:245
  29.5 22.7 %collective-permute-start.6 = (bf16[352,512]{1,0:T(8,128)(2,1)S(1)}, bf16[352,512]{1,0:T(8,128)(2,1)S(1)}, u32[]{:S(2)}, u32[]{:S(2)}) collective-permute-start(bf16[352,512]{1,0:T(8,128)(2,1)S(1)} %slice.150), channel_id=1, source_target_pairs={{0,1},{1,2},{2,3},{3,0},{4,5},{5,6},{6,7},{7,4},{8,9},{9,10},{10,1... | collective-permute-start | bytes 1081352 | tf_op jit(solution)/shard_map/cond/branch_0_fun/ppermute | solution.py:245
  41.4 15.4 %collective-permute-start.5 = (bf16[352,512]{1,0:T(8,128)(2,1)S(1)}, bf16[352,512]{1,0:T(8,128)(2,1)S(1)}, u32[]{:S(2)}, u32[]{:S(2)}) collective-permute-start(bf16[352,512]{1,0:T(8,128)(2,1)S(1)} %slice.149), channel_id=1, source_target_pairs={{0,3},{1,0},{2,1},{3,2},{4,7},{5,4},{6,5},{7,6},{8,11},{9,8},{10,9... | collective-permute-start | bytes 1081352 | tf_op jit(solution)/shard_map/cond/branch_0_fun/ppermute | solution.py:245
  45.0 15.0 %collective-permute-start.4 = (bf16[352,512]{1,0:T(8,128)(2,1)S(1)}, bf16[352,512]{1,0:T(8,128)(2,1)S(1)}, u32[]{:S(2)}, u32[]{:S(2)}) collective-permute-start(bf16[352,512]{1,0:T(8,128)(2,1)S(1)} %slice.148), channel_id=1, source_target_pairs={{0,1},{1,2},{2,3},{3,0},{4,5},{5,6},{6,7},{7,4},{8,9},{9,10},{10,1... | collective-permute-start | bytes 1081352 | tf_op jit(solution)/shard_map/cond/branch_0_fun/ppermute | solution.py:245
where the time goes:
time: 191 us
  blocking collectives  99.8 us (52%)
  waiting for transfers between devices  38.8 us (20%)
  Pallas kernels  36 us (19%)
  starting transfers between devices  13.4 us (7%)
    all_to_all x1, blocking collectives, on_device(): lax.all_to_all(context.reshape(shards, count, 4 * width + HD), 'dp', 0, 0...  56.6 us
    all_to_all x1, blocking collectives, on_device(): lax.all_to_all(routed.reshape(shards, GCAP, 4 * width), 'dp', 0, 0, tiled...  43.2 us
    ppermute x8, waiting for transfers between devices, gather(): lax.ppermute(x, 'mp', [(i, (i + step) % 4) for i in range(4)])  38.8 us
    pallas_call x1, Pallas kernels, attend(): pl.pallas_call(attend_kernel, out_shape=jax.ShapeDtypeStruct((n, 4 * widt...  23.3 us
    ppermute x8, starting transfers between devices, gather(): lax.ppermute(x, 'mp', [(i, (i + step) % 4) for i in range(4)])  13.4 us
    pallas_call x1, Pallas kernels, on_device(): pl.pallas_call(pack_kernel, out_shape=[jax.ShapeDtypeStruct((5, count), j...  5.25 us
  transfers between devices with their start and end apart: 8, of which 6 were waited for; matrix products, arithmetic and copies ran while one was open for 0% of the time, Pallas kernels for 0%

commit v1 on v0

--- a/solution.py
+++ b/solution.py
@@ -15,13 +15,13 @@
 BLOCK = 16
 BLOCKS = L // BLOCK
 TILE = 256
-SIZES = (1408, 1536, 1664, 1792, 1920, 2048, 2304, 4096)
+SIZES = (1408, 1536, 1664, 1728, 1792, 1856, 1920, 2048, 2304, 4096)
 VMEM = pl.BlockSpec(memory_space=pltpu.VMEM)
 SMEM = pl.BlockSpec(memory_space=pltpu.SMEM)
 HBM = pl.BlockSpec(memory_space=pltpu.HBM)
 
 
-def pack_kernel(cand, lens, enc, dec, out_pairs, facts, out, staged, starts, arrived):
+def pack_kernel(cand, lens, enc, dec, out_pairs, facts, out_hbm, out, staged, starts, arrived, left):
     rows = enc.shape[0] // L
     count = cand.shape[1]
     for row in range(rows):
@@ -87,14 +87,28 @@
 
     lax.fori_loop(total, size // BLOCK, clear, 0)
 
+    def leave(i):
+        rows = pl.ds(pl.multiple_of(i * L, L), L)
+        return pltpu.make_async_copy(out.at[rows], out_hbm.at[rows], left.at[i])
+
+    def begin_leave(i, carry):
+        leave(i).start()
+        return carry
+
+    def finish_leave(i, carry):
+        leave(i).wait()
+        return carry
+
+    pieces = (size + L - 1) // L
+    lax.fori_loop(0, pieces, begin_leave, 0)
+    lax.fori_loop(0, pieces, finish_leave, 0)
+
 
 def assemble_kernel(*refs):
-    pieces, (out1, out2, out3, done) = refs[:8], refs[8:]
+    pieces, (out1, out2, out3, done) = refs[:6], refs[6:]
     half = pieces[0].shape[0]
-    quarter = half // 2
-    outs = (out1.at[:half], out3.at[:half], out1.at[half : 2 * half], out3.at[half : 2 * half]) + tuple(
-        out2.at[k * quarter : (k + 1) * quarter] for k in range(4)
-    )
+    low, high = slice(0, half), slice(half, 2 * half)
+    outs = (out1.at[low], out3.at[high], out1.at[high], out3.at[low], out2.at[low], out2.at[high])
     copies = [pltpu.make_async_copy(piece, out, done.at[k]) for k, (piece, out) in enumerate(zip(pieces, outs))]
     for copy in copies:
         copy.start()
@@ -102,7 +116,9 @@
         copy.wait()
 
 
-def attend_kernel(facts, pairs, x0, x1, x2, x3, wq, wk, wv, out, xs, keys, values, queries, turned, arrived):
+def attend_kernel(
+    facts, pairs, x0, x1, x2, x3, wq_in, wk, wv_in, out, xs, wq, wv, keys, values, queries, turned, arrived, ready
+):
     width = x0.shape[1]
     heads = width // HD
     me = lax.axis_index("mp")
@@ -129,34 +145,45 @@
             copy.wait()
         return carry
 
-    lax.fori_loop(0, chunks, begin, 0)
-
-    def kv_tile(i, carry):
+    value_load = pltpu.make_async_copy(wv_in, wv, ready.at[0])
+    query_load = pltpu.make_async_copy(wq_in, wq, ready.at[1])
+    begin(0, 0)
+    value_load.start()
+    lax.fori_loop(1, chunks, begin, 0)
+    query_load.start()
+
+    def project(i, weight, out):
+        rows = pl.ds(pl.multiple_of(i * TILE, TILE), TILE)
+        total = jnp.zeros((TILE, width), jnp.float32)
+        for d in range(4):
+            total += jnp.dot(xs[d, rows, :], weight[pl.ds(origin[d], width), :], preferred_element_type=jnp.float32)
+        out[rows, :] = total.astype(jnp.bfloat16)
+
+    def key_tile(i, carry):
         finish(i, 0)
-        rows = pl.ds(pl.multiple_of(i * TILE, TILE), TILE)
-        key_sum = jnp.zeros((TILE, width), jnp.float32)
-        value_sum = jnp.zeros((TILE, width), jnp.float32)
-        for d in range(4):
-            x = xs[d, rows, :]
-            key_sum += jnp.dot(x, wk[pl.ds(origin[d], width), :], preferred_element_type=jnp.float32)
-            value_sum += jnp.dot(x, wv[pl.ds(origin[d], width), :], preferred_element_type=jnp.float32)
-        keys[rows, :] = key_sum.astype(jnp.bfloat16)
-        values[rows, :] = value_sum.astype(jnp.bfloat16)
-        return carry
-
-    lax.fori_loop(0, tiles, kv_tile, 0)
+        project(i, wk, keys)
+        return carry
+
+    def value_tile(i, carry):
+        project(i, wv, values)
+        return carry
+
+    lax.fori_loop(0, tiles, key_tile, 0)
+    value_load.wait()
+    lax.fori_loop(0, tiles, value_tile, 0)
     values[pl.ds(source, L), :] = jnp.zeros((L, width), jnp.bfloat16)
     lax.fori_loop(tiles, chunks, finish, 0)
+    query_load.wait()
 
     def q_tile(i, carry):
         rows = pl.ds(pl.multiple_of(source + i * TILE, BLOCK), TILE)
-        parts = [xs[d, rows, :].astype(jnp.float32) for d in range(4)]
-        mean = sum(jnp.sum(x, axis=-1, keepdims=True) for x in parts) * (1.0 / D)
-        parts = [x - mean for x in parts]
-        variance = sum(jnp.sum(x * x, axis=-1, keepdims=True) for x in parts) * (1.0 / D)
+        wide = [xs[d, rows, :].astype(jnp.float32) for d in range(4)]
+        mean = sum(jnp.sum(x, axis=-1, keepdims=True) for x in wide) * (1.0 / D)
+        wide = [x - mean for x in wide]
+        variance = sum(jnp.sum(x * x, axis=-1, keepdims=True) for x in wide) * (1.0 / D)
         scale = lax.rsqrt(variance + 1e-05)
         total = jnp.zeros((TILE, width), jnp.float32)
-        for x, start in zip(parts, origin):
+        for x, start in zip(wide, origin):
             total += jnp.dot(
                 (x * scale).astype(jnp.bfloat16), wq[pl.ds(start, width), :], preferred_element_type=jnp.float32
             )
@@ -197,7 +224,7 @@
                 turned[h + g * heads, pl.ds(p, 32, stride=count), :] = context[g * 32 : (g + 1) * 32]
         return carry
 
-    lax.fori_loop(0, count, pair, 0)
+    lax.fori_loop(0, count, pair, 0, unroll=4)
     for k in range(4 * heads):
         g, h = k // heads, k % heads
         at = g * width + h * HD
@@ -241,42 +268,42 @@
 
 
 def gather(size, packed):
-    half, quarter = size // 2, size // 4
+    half = size // 2
     send = lambda x, step: lax.ppermute(x, "mp", [(i, (i + step) % 4) for i in range(4)])
-    direct, across = [], []
-    for c in range(2):
-        own = packed[c * half : (c + 1) * half]
-        direct += [send(own, 1), send(own, 3)]
-    for c in range(2):
-        across += [send(direct[2 * c][:quarter], 1), send(direct[2 * c + 1][quarter:], 3)]
+    low, high = packed[:half], packed[half:size]
+    left, right = send(low, 1), send(high, 3)
+    pieces = [left, right, send(high, 1), send(low, 3), send(left, 1), send(right, 3)]
     return pl.pallas_call(
         assemble_kernel,
         out_shape=[jax.ShapeDtypeStruct(packed.shape, jnp.bfloat16)] * 3,
-        in_specs=[VMEM] * 8,
+        in_specs=[VMEM] * 6,
         out_specs=[HBM] * 3,
-        scratch_shapes=[pltpu.SemaphoreType.DMA((8,))],
+        scratch_shapes=[pltpu.SemaphoreType.DMA((6,))],
         compiler_params=pltpu.CompilerParams(vmem_limit_bytes=13 * 2**20),
-    )(*direct, *across)
+    )(*pieces)
 
 
 def attend(facts, pairs, x0, x1, x2, x3, wq, wk, wv):
     total, width = x0.shape
-    rows = total // 2
+    rows = total // 2 - TILE // 2
     n = pairs.shape[1] * 32
     return pl.pallas_call(
         attend_kernel,
         out_shape=jax.ShapeDtypeStruct((n, 4 * width + HD), jnp.bfloat16),
-        in_specs=[SMEM, SMEM, VMEM] + [HBM] * 3 + [VMEM] * 3,
+        in_specs=[SMEM, SMEM] + [HBM] * 5 + [VMEM, HBM],
         out_specs=VMEM,
         scratch_shapes=[
-            pltpu.VMEM((4, total + TILE, width), jnp.bfloat16),
+            pltpu.VMEM((4, total, width), jnp.bfloat16),
+            pltpu.VMEM((D, width), jnp.bfloat16),
+            pltpu.VMEM((D, width), jnp.bfloat16),
             pltpu.VMEM((rows + L, width), jnp.bfloat16),
             pltpu.VMEM((rows + L, width), jnp.bfloat16),
             pltpu.VMEM((rows + L, width), jnp.bfloat16),
             pltpu.VMEM((4 * width // HD, n, HD), jnp.float32),
             pltpu.SemaphoreType.DMA((4, total // TILE)),
+            pltpu.SemaphoreType.DMA((2,)),
         ],
-        compiler_params=pltpu.CompilerParams(vmem_limit_bytes=50 * 2**20),
+        compiler_params=pltpu.CompilerParams(vmem_limit_bytes=54 * 2**20),
     )(facts, pairs, x0, x1, x2, x3, wq, wk, wv)
 
 
@@ -291,14 +318,16 @@
         out_shape=[
             jax.ShapeDtypeStruct((5, count), jnp.int32),
             jax.ShapeDtypeStruct((3,), jnp.int32),
-            jax.ShapeDtypeStruct((2 * rows, width), jnp.bfloat16),
+            jax.ShapeDtypeStruct((2 * rows + TILE, width), jnp.bfloat16),
         ],
         in_specs=[SMEM, SMEM, HBM, HBM],
-        out_specs=[SMEM, SMEM, VMEM],
+        out_specs=[SMEM, SMEM, HBM],
         scratch_shapes=[
+            pltpu.VMEM((2 * rows + TILE, width), jnp.bfloat16),
             pltpu.VMEM((2, rows, width), jnp.bfloat16),
             pltpu.SMEM((2, bank), jnp.int32),
             pltpu.SemaphoreType.DMA((2, bank)),
+            pltpu.SemaphoreType.DMA((2 * bank + TILE // L,)),
         ],
         compiler_params=pltpu.CompilerParams(vmem_limit_bytes=58 * 2**20),
     )(candidates.T, row_lengths.T, enc_bank.reshape(rows, width), dec_bank.reshape(rows, width))

time: 191 us -> 184 us (0.963); the launches traced: 191 us -> 181 us
  blocking collectives: 99.8 us -> 92.5 us
  waiting for transfers between devices: 38.8 us -> 42.5 us
  starting transfers between devices: 13.4 us -> 9.76 us
  Pallas kernels: 36 us -> 33.3 us
    all_to_all x1, blocking collectives: 56.6 us -> 49.2 us  [on_device(): lax.all_to_all(context.reshape(shards, count, 4 * width + HD), 'dp', 0, 0...]
    ppermute x8 -> x6, starting transfers between devices: 13.4 us -> 9.76 us  [gather(): lax.ppermute(x, 'mp', [(i, (i + step) % 4) for i in range(4)])]
    ppermute x8 -> x6, waiting for transfers between devices: 38.8 us -> 42.5 us  [gather(): lax.ppermute(x, 'mp', [(i, (i + step) % 4) for i in range(4)])]
    pallas_call x1, Pallas kernels: 23.3 us -> 20.6 us  [attend(): pl.pallas_call(attend_kernel, out_shape=jax.ShapeDtypeStruct((n, 4 * widt...]
  transfers between devices with their start and end apart: 8 -> 6, of which waited for: 6 -> 4; matrix products, arithmetic and copies ran while one was open for 0% -> 0% of each run, Pallas kernels for 0% -> 0%
where the time goes in v1:
time: 184 us; the launch traced here: 181 us
  blocking collectives  92.5 us (50%)
  waiting for transfers between devices  42.5 us (23%)
  Pallas kernels  33.3 us (18%)
  starting transfers between devices  9.76 us (5%)
    all_to_all x1, blocking collectives, on_device(): lax.all_to_all(context.reshape(shards, count, 4 * width + HD), 'dp', 0, 0...  49.2 us
    all_to_all x1, blocking collectives, on_device(): lax.all_to_all(routed.reshape(shards, GCAP, 4 * width), 'dp', 0, 0, tiled...  43.2 us
    ppermute x6, waiting for transfers between devices, gather(): lax.ppermute(x, 'mp', [(i, (i + step) % 4) for i in range(4)])  42.5 us
    pallas_call x1, Pallas kernels, attend(): pl.pallas_call(attend_kernel, out_shape=jax.ShapeDtypeStruct((n, 4 * widt...  20.6 us
    ppermute x6, starting transfers between devices, gather(): lax.ppermute(x, 'mp', [(i, (i + step) % 4) for i in range(4)])  9.76 us
    pallas_call x1, Pallas kernels, on_device(): pl.pallas_call(pack_kernel, out_shape=[jax.ShapeDtypeStruct((5, count), j...  5.31 us
  transfers between devices with their start and end apart: 6, of which 4 were waited for; matrix products, arithmetic and copies ran while one was open for 0% of the time, Pallas kernels for 0%

profile of v1, /device:TPU:1, one launch (start us, length us, event | category | flops | bytes accessed | tf_op | source)
XLA Modules:
  0.0 180.6 jit_solution(12829456197530285817)
XLA Ops:
  0.0 5.3 %shard_map.73 = (s32[5,16]{1,0:T(8,128)}, s32[3]{0:T(128)}, bf16[4352,512]{1,0:T(8,128)(2,1)}) custom-call(s32[3,16]{1,0:T(4,128)} %bitcast.17, s32[2,16]{1,0:T(2,128)} %bitcast.18, bf16[2048,512]{1,0:T(8,128)(2,1)} %bitcast.14, bf16[2048,512]{1,0:T(8,128)(2,1)} %bitcast.15), custom_call_target="tpu_custom_call" | custom-call | tf_op jit(solution)/shard_map/pallas_call | solution.py:316
  6.0 56.2 %conditional.1 = ((bf16[4352,512]{1,0:T(8,128)(2,1)}, bf16[4352,512]{1,0:T(8,128)(2,1)}, bf16[4352,512]{1,0:T(8,128)(2,1)})) conditional(s32[]{:T(128)} %bitcast.4, bf16[4352,512]{1,0:T(8,128)(2,1)} %get-tuple-element.23.x0, bf16[4352,512]{1,0:T(8,128)(2,1)} %get-tuple-element.23.x0, ...), branch_computations={%region_0.0_spmd, %region_1.0_spmd, %region_2.0_spmd, %region_3.0_... | conditional | bytes 58720504 | solution.py:334
  6.0 1.4 fusion
  7.4 3.6 %collective-permute-start.1 = (bf16[704,512]{1,0:T(8,128)(2,1)S(1)}, bf16[704,512]{1,0:T(8,128)(2,1)S(1)}, u32[]{:S(2)}, u32[]{:S(2)}) collective-permute-start(bf16[704,512]{1,0:T(8,128)(2,1)S(1)} %get-tuple-element.27), channel_id=1, source_target_pairs={{0,3},{1,0},{2,1},{3,2},{4,7},{5,4},{6,5},{7,6},{8,11},{9,8},{10,9... | collective-permute-start | bytes 2162696 | tf_op jit(solution)/shard_map/cond/branch_0_fun/ppermute | solution.py:272
  11.1 0.0 collective-permute-start
  11.1 0.0 collective-permute-start.2
  11.1 2.7 %collective-permute-start.3 = (bf16[704,512]{1,0:T(8,128)(2,1)S(1)}, bf16[704,512]{1,0:T(8,128)(2,1)S(1)}, u32[]{:S(2)}, u32[]{:S(2)}) collective-permute-start(bf16[704,512]{1,0:T(8,128)(2,1)S(1)} %get-tuple-element.28), channel_id=1, source_target_pairs={{0,3},{1,0},{2,1},{3,2},{4,7},{5,4},{6,5},{7,6},{8,11},{9,8},{10,9... | collective-permute-start | bytes 2162696 | tf_op jit(solution)/shard_map/cond/branch_0_fun/ppermute | solution.py:272
  13.8 11.9 %collective-permute-done.1.refs_1_ = bf16[704,512]{1,0:T(8,128)(2,1)S(1)} collective-permute-done((bf16[704,512]{1,0:T(8,128)(2,1)S(1)}, bf16[704,512]{1,0:T(8,128)(2,1)S(1)}, u32[]{:S(2)}, u32[]{:S(2)}) %collective-permute-start.1) | collective-permute-done | bytes 720928 | tf_op jit(solution)/shard_map/cond/branch_0_fun/ppermute | solution.py:272
  25.7 3.4 %collective-permute-start.5 = (bf16[704,512]{1,0:T(8,128)(2,1)S(1)}, bf16[704,512]{1,0:T(8,128)(2,1)S(1)}, u32[]{:S(2)}, u32[]{:S(2)}) collective-permute-start(bf16[704,512]{1,0:T(8,128)(2,1)S(1)} %collective-permute-done.1.refs_1_), channel_id=1, source_target_pairs={{0,3},{1,0},{2,1},{3,2},{4,7},{5,4},{6,5},{7,6},{8,11},{9,8},{10,9... | collective-permute-start | bytes 2162696 | tf_op jit(solution)/shard_map/cond/branch_0_fun/ppermute | solution.py:272
  29.1 0.0 collective-permute-done.refs_0_
  29.1 0.0 collective-permute-start.4
  29.1 15.1 %collective-permute-done.2.refs_2_ = bf16[704,512]{1,0:T(8,128)(2,1)S(1)} collective-permute-done((bf16[704,512]{1,0:T(8,128)(2,1)S(1)}, bf16[704,512]{1,0:T(8,128)(2,1)S(1)}, u32[]{:S(2)}, u32[]{:S(2)}) %collective-permute-start.2) | collective-permute-done | bytes 720928 | tf_op jit(solution)/shard_map/cond/branch_0_fun/ppermute | solution.py:272
  44.2 0.0 collective-permute-done.3.refs_3_
  44.2 12.3 %collective-permute-done.5.refs_5_ = bf16[704,512]{1,0:T(8,128)(2,1)S(1)} collective-permute-done((bf16[704,512]{1,0:T(8,128)(2,1)S(1)}, bf16[704,512]{1,0:T(8,128)(2,1)S(1)}, u32[]{:S(2)}, u32[]{:S(2)}) %collective-permute-start.5) | collective-permute-done | bytes 720928 | tf_op jit(solution)/shard_map/cond/branch_0_fun/ppermute | solution.py:272
  56.6 3.1 %collective-permute-done.4.refs_4_ = bf16[704,512]{1,0:T(8,128)(2,1)S(1)} collective-permute-done((bf16[704,512]{1,0:T(8,128)(2,1)S(1)}, bf16[704,512]{1,0:T(8,128)(2,1)S(1)}, u32[]{:S(2)}, u32[]{:S(2)}) %collective-permute-start.4) | collective-permute-done | bytes 720928 | tf_op jit(solution)/shard_map/cond/branch_0_fun/ppermute | solution.py:272
  59.7 2.1 %branch_0_fun.1 = (bf16[4352,512]{1,0:T(8,128)(2,1)}, bf16[4352,512]{1,0:T(8,128)(2,1)}, bf16[4352,512]{1,0:T(8,128)(2,1)}) custom-call(bf16[704,512]{1,0:T(8,128)(2,1)S(1)} %collective-permute-done.refs_0_, bf16[704,512]{1,0:T(8,128)(2,1)S(1)} %collective-permute-done.1.refs_1_, bf16[704,512]{1,0:T(8,128)(2,1)S(1)} %collective-permute-done.2.refs_2_, ...), custom_call_target="tpu_custom_call" | custom-call | tf_op jit(solution)/shard_map/cond/branch_0_fun/pallas_call | solution.py:276
  62.2 20.6 %shard_map.74 = bf16[512,2176]{1,0:T(8,128)(2,1)} custom-call(s32[3]{0:T(128)} %get-tuple-element.21.facts, s32[5,16]{1,0:T(8,128)} %get-tuple-element.22.pairs, bf16[4352,512]{1,0:T(8,128)(2,1)} %get-tuple-element.23.x0, bf16[4352,512]{1,0:T(8,128)(2,1)} %get-tuple-element.24.x1, bf16[4352,512]{1,0:T(8,128)(2,1)} %get-tuple-element.25.x2, ...), custom_call_target="tpu_custom_call" | custom-call | tf_op jit(solution)/shard_map/pallas_call | solution.py:290
  82.7 49.2 %all_to_all.10 = bf16[32,16,2176]{2,1,0:T(8,128)(2,1)S(1)} all-to-all(bf16[32,16,2176]{2,1,0:T(8,128)(2,1)} %bitcast.13), channel_id=1, replica_groups=mesh['dp'=32,'mp'=4] {'dp'}, dimensions={0} | all-to-all | bytes 4456448 | tf_op jit(solution)/shard_map/all_to_all | solution.py:336
  132.0 2.2 %shard_map.75 = bf16[768,2048]{1,0:T(8,128)(2,1)S(1)} custom-call(bf16[512,2176]{1,0:T(8,128)(2,1)S(1)} %bitcast.12), custom_call_target="tpu_custom_call" | custom-call | tf_op jit(solution)/shard_map/pallas_call | solution.py:337
  134.2 43.2 %all_to_all.11 = bf16[32,24,2048]{2,1,0:T(8,128)(2,1)S(1)} all-to-all(bf16[32,24,2048]{2,1,0:T(8,128)(2,1)S(1)} %bitcast.11), channel_id=1, replica_groups=mesh['dp'=32,'mp'=4] {'dp'}, dimensions={0} | all-to-all | bytes 6291456 | tf_op jit(solution)/shard_map/all_to_all | solution.py:344
  177.4 3.2 %shard_map.76 = bf16[24,128,512]{2,1,0:T(8,128)(2,1)} custom-call(bf16[768,2048]{1,0:T(8,128)(2,1)S(1)} %bitcast.10), custom_call_target="tpu_custom_call" | custom-call | tf_op jit(solution)/shard_map/pallas_call | solution.py:345
Async XLA Ops:
  7.4 18.2 %collective-permute-start.1 = (bf16[704,512]{1,0:T(8,128)(2,1)S(1)}, bf16[704,512]{1,0:T(8,128)(2,1)S(1)}, u32[]{:S(2)}, u32[]{:S(2)}) collective-permute-start(bf16[704,512]{1,0:T(8,128)(2,1)S(1)} %get-tuple-element.27), channel_id=1, source_target_pairs={{0,3},{1,0},{2,1},{3,2},{4,7},{5,4},{6,5},{7,6},{8,11},{9,8},{10,9... | collective-permute-start | bytes 2162696 | tf_op jit(solution)/shard_map/cond/branch_0_fun/ppermute | solution.py:272
  11.1 18.0 %collective-permute-start = (bf16[704,512]{1,0:T(8,128)(2,1)S(1)}, bf16[704,512]{1,0:T(8,128)(2,1)S(1)}, u32[]{:S(2)}, u32[]{:S(2)}) collective-permute-start(bf16[704,512]{1,0:T(8,128)(2,1)S(1)} %get-tuple-element.28), channel_id=1, source_target_pairs={{0,1},{1,2},{2,3},{3,0},{4,5},{5,6},{6,7},{7,4},{8,9},{9,10},{10,1... | collective-permute-start | bytes 2162696 | tf_op jit(solution)/shard_map/cond/branch_0_fun/ppermute | solution.py:272
  11.1 33.2 %collective-permute-start.2 = (bf16[704,512]{1,0:T(8,128)(2,1)S(1)}, bf16[704,512]{1,0:T(8,128)(2,1)S(1)}, u32[]{:S(2)}, u32[]{:S(2)}) collective-permute-start(bf16[704,512]{1,0:T(8,128)(2,1)S(1)} %get-tuple-element.27), channel_id=1, source_target_pairs={{0,1},{1,2},{2,3},{3,0},{4,5},{5,6},{6,7},{7,4},{8,9},{9,10},{10,1... | collective-permute-start | bytes 2162696 | tf_op jit(solution)/shard_map/cond/branch_0_fun/ppermute | solution.py:272
  11.1 33.1 %collective-permute-start.3 = (bf16[704,512]{1,0:T(8,128)(2,1)S(1)}, bf16[704,512]{1,0:T(8,128)(2,1)S(1)}, u32[]{:S(2)}, u32[]{:S(2)}) collective-permute-start(bf16[704,512]{1,0:T(8,128)(2,1)S(1)} %get-tuple-element.28), channel_id=1, source_target_pairs={{0,3},{1,0},{2,1},{3,2},{4,7},{5,4},{6,5},{7,6},{8,11},{9,8},{10,9... | collective-permute-start | bytes 2162696 | tf_op jit(solution)/shard_map/cond/branch_0_fun/ppermute | solution.py:272
  25.7 30.9 %collective-permute-start.5 = (bf16[704,512]{1,0:T(8,128)(2,1)S(1)}, bf16[704,512]{1,0:T(8,128)(2,1)S(1)}, u32[]{:S(2)}, u32[]{:S(2)}) collective-permute-start(bf16[704,512]{1,0:T(8,128)(2,1)S(1)} %collective-permute-done.1.refs_1_), channel_id=1, source_target_pairs={{0,3},{1,0},{2,1},{3,2},{4,7},{5,4},{6,5},{7,6},{8,11},{9,8},{10,9... | collective-permute-start | bytes 2162696 | tf_op jit(solution)/shard_map/cond/branch_0_fun/ppermute | solution.py:272
  29.1 30.6 %collective-permute-start.4 = (bf16[704,512]{1,0:T(8,128)(2,1)S(1)}, bf16[704,512]{1,0:T(8,128)(2,1)S(1)}, u32[]{:S(2)}, u32[]{:S(2)}) collective-permute-start(bf16[704,512]{1,0:T(8,128)(2,1)S(1)} %collective-permute-done.refs_0_), channel_id=1, source_target_pairs={{0,1},{1,2},{2,3},{3,0},{4,5},{5,6},{6,7},{7,4},{8,9},{9,10},{10,1... | collective-permute-start | bytes 2162696 | tf_op jit(solution)/shard_map/cond/branch_0_fun/ppermute | solution.py:272

commit v2 on v1

--- a/solution.py
+++ b/solution.py
@@ -21,7 +21,7 @@
 HBM = pl.BlockSpec(memory_space=pltpu.HBM)
 
 
-def pack_kernel(cand, lens, enc, dec, out_pairs, facts, out_hbm, out, staged, starts, arrived, left):
+def pack_kernel(cand, lens, enc, dec, out_pairs, facts, out, out_hbm, staged, starts, arrived, left):
     rows = enc.shape[0] // L
     count = cand.shape[1]
     for row in range(rows):
@@ -51,15 +51,11 @@
             starts[column, row] = total * BLOCK
 
             @pl.when(needed)
-            def _(column=column, row=row):
+            def _(column=column, row=row, first=total):
                 load(column, row).wait()
-
-            def move(b, carry, column=column, row=row, first=total):
-                to = pl.multiple_of((first + b) * BLOCK, BLOCK)
-                out[pl.ds(to, BLOCK), :] = staged[column, pl.ds(pl.multiple_of(row * L + b * BLOCK, BLOCK), BLOCK), :]
-                return carry
-
-            lax.fori_loop(0, blocks, move, 0)
+                to = pl.multiple_of(first * BLOCK, BLOCK)
+                out[pl.ds(to, L), :] = staged[column, row * L : (row + 1) * L, :]
+
             total = total + blocks
         facts[1 + column] = total * BLOCK
     bucket = jnp.int32(0)
@@ -80,12 +76,6 @@
         return carry
 
     lax.fori_loop(0, count, place, 0)
-
-    def clear(b, carry):
-        out[pl.ds(pl.multiple_of(b * BLOCK, BLOCK), BLOCK), :] = jnp.zeros((BLOCK, out.shape[1]), out.dtype)
-        return carry
-
-    lax.fori_loop(total, size // BLOCK, clear, 0)
 
     def leave(i):
         rows = pl.ds(pl.multiple_of(i * L, L), L)
@@ -117,7 +107,7 @@
 
 
 def attend_kernel(
-    facts, pairs, x0, x1, x2, x3, wq_in, wk, wv_in, out, xs, wq, wv, keys, values, queries, turned, arrived, ready
+    facts, pairs, x0, x1, x2, x3, wk, wv_in, wq_in, out, xs, wq, wv, keys, values, queries, turned, arrived, ready
 ):
     width = x0.shape[1]
     heads = width // HD
@@ -290,7 +280,7 @@
     return pl.pallas_call(
         attend_kernel,
         out_shape=jax.ShapeDtypeStruct((n, 4 * width + HD), jnp.bfloat16),
-        in_specs=[SMEM, SMEM] + [HBM] * 5 + [VMEM, HBM],
+        in_specs=[SMEM, SMEM] + [HBM] * 4 + [VMEM, HBM, HBM],
         out_specs=VMEM,
         scratch_shapes=[
             pltpu.VMEM((4, total, width), jnp.bfloat16),
@@ -304,7 +294,7 @@
             pltpu.SemaphoreType.DMA((2,)),
         ],
         compiler_params=pltpu.CompilerParams(vmem_limit_bytes=54 * 2**20),
-    )(facts, pairs, x0, x1, x2, x3, wq, wk, wv)
+    )(facts, pairs, x0, x1, x2, x3, wk, wv, wq)
 
 
 def on_device(candidates, row_lengths, enc_bank, dec_bank, w_query, w_key, w_value):
@@ -313,17 +303,17 @@
     bank = enc_bank.shape[0]
     width = enc_bank.shape[2]
     rows = bank * L
-    pairs, facts, packed = pl.pallas_call(
+    pairs, facts, packed, kept = pl.pallas_call(
         pack_kernel,
         out_shape=[
             jax.ShapeDtypeStruct((5, count), jnp.int32),
             jax.ShapeDtypeStruct((3,), jnp.int32),
             jax.ShapeDtypeStruct((2 * rows + TILE, width), jnp.bfloat16),
+            jax.ShapeDtypeStruct((2 * rows + TILE, width), jnp.bfloat16),
         ],
         in_specs=[SMEM, SMEM, HBM, HBM],
-        out_specs=[SMEM, SMEM, HBM],
+        out_specs=[SMEM, SMEM, VMEM, HBM],
         scratch_shapes=[
-            pltpu.VMEM((2 * rows + TILE, width), jnp.bfloat16),
             pltpu.VMEM((2, rows, width), jnp.bfloat16),
             pltpu.SMEM((2, bank), jnp.int32),
             pltpu.SemaphoreType.DMA((2, bank)),
@@ -332,7 +322,7 @@
         compiler_params=pltpu.CompilerParams(vmem_limit_bytes=58 * 2**20),
     )(candidates.T, row_lengths.T, enc_bank.reshape(rows, width), dec_bank.reshape(rows, width))
     x1, x2, x3 = lax.switch(facts[0], [functools.partial(gather, size) for size in SIZES], packed)
-    context = attend(facts, pairs, packed, x1, x2, x3, w_query, w_key, w_value)
+    context = attend(facts, pairs, kept, x1, x2, x3, w_query, w_key, w_value)
     spread = lax.all_to_all(context.reshape(shards, count, 4 * width + HD), "dp", 0, 0, tiled=True)
     routed = pl.pallas_call(
         route_kernel,

time: 184 us -> 183 us (level); the launches traced: 181 us -> 183 us
  waiting for transfers between devices: 42.5 us -> 46.8 us
    ppermute x6, waiting for transfers between devices: 42.5 us -> 46.8 us  [gather(): lax.ppermute(x, 'mp', [(i, (i + step) % 4) for i in range(4)])]
where the time goes in v2:
time: 183 us
  blocking collectives  91.1 us (50%)
  waiting for transfers between devices  46.8 us (26%)
  Pallas kernels  34.4 us (19%)
  starting transfers between devices  9.76 us (5%)
    all_to_all x1, blocking collectives, on_device(): lax.all_to_all(context.reshape(shards, count, 4 * width + HD), 'dp', 0, 0...  47.8 us
    ppermute x6, waiting for transfers between devices, gather(): lax.ppermute(x, 'mp', [(i, (i + step) % 4) for i in range(4)])  46.8 us
    all_to_all x1, blocking collectives, on_device(): lax.all_to_all(routed.reshape(shards, GCAP, 4 * width), 'dp', 0, 0, tiled...  43.2 us
    pallas_call x1, Pallas kernels, attend(): pl.pallas_call(attend_kernel, out_shape=jax.ShapeDtypeStruct((n, 4 * widt...  21.7 us
    ppermute x6, starting transfers between devices, gather(): lax.ppermute(x, 'mp', [(i, (i + step) % 4) for i in range(4)])  9.76 us
    pallas_call x1, Pallas kernels, on_device(): pl.pallas_call(pack_kernel, out_shape=[jax.ShapeDtypeStruct((5, count), j...  5.17 us
  transfers between devices with their start and end apart: 6, of which 4 were waited for; matrix products, arithmetic and copies ran while one was open for 0% of the time, Pallas kernels for 0%

profile of v2, /device:TPU:1, one launch (start us, length us, event | category | flops | bytes accessed | tf_op | source)
XLA Modules:
  0.0 183.3 jit_solution(17335015051427599575)
XLA Ops:
  0.0 5.2 %shard_map.73 = (s32[5,16]{1,0:T(8,128)}, s32[3]{0:T(128)}, bf16[4352,512]{1,0:T(8,128)(2,1)S(1)}, bf16[4352,512]{1,0:T(8,128)(2,1)}) custom-call(s32[3,16]{1,0:T(4,128)} %bitcast.17, s32[2,16]{1,0:T(2,128)} %bitcast.18, bf16[2048,512]{1,0:T(8,128)(2,1)} %bitcast.14, bf16[2048,512]{1,0:T(8,128)(2,1)} %bitcast.15), custom_call_target="tpu_custom_call" | custom-call | tf_op jit(solution)/shard_map/pallas_call | solution.py:306
  5.8 59.3 %conditional.1 = ((bf16[4352,512]{1,0:T(8,128)(2,1)}, bf16[4352,512]{1,0:T(8,128)(2,1)}, bf16[4352,512]{1,0:T(8,128)(2,1)})) conditional(s32[]{:T(128)} %bitcast.4, bf16[4352,512]{1,0:T(8,128)(2,1)S(1)} %get-tuple-element.25, bf16[4352,512]{1,0:T(8,128)(2,1)S(1)} %get-tuple-element.25, ...), branch_computations={%region_0.0_spmd, %region_1.0_spmd, %region_2.0_spmd, %region_3.0_... | conditional | bytes 58720504 | solution.py:324
  5.9 0.1 fusion.1
  6.0 3.6 %collective-permute-start.7 = (bf16[768,512]{1,0:T(8,128)(2,1)S(1)}, bf16[768,512]{1,0:T(8,128)(2,1)S(1)}, u32[]{:S(2)}, u32[]{:S(2)}) collective-permute-start(bf16[768,512]{1,0:T(8,128)(2,1)S(1)} %get-tuple-element.31), channel_id=1, source_target_pairs={{0,3},{1,0},{2,1},{3,2},{4,7},{5,4},{6,5},{7,6},{8,11},{9,8},{10,9... | collective-permute-start | bytes 2359304 | tf_op jit(solution)/shard_map/cond/branch_1_fun/ppermute | solution.py:262
  9.6 0.0 collective-permute-start.6
  9.6 0.0 collective-permute-start.8
  9.7 2.7 %collective-permute-start.9 = (bf16[768,512]{1,0:T(8,128)(2,1)S(1)}, bf16[768,512]{1,0:T(8,128)(2,1)S(1)}, u32[]{:S(2)}, u32[]{:S(2)}) collective-permute-start(bf16[768,512]{1,0:T(8,128)(2,1)S(1)} %get-tuple-element.32), channel_id=1, source_target_pairs={{0,3},{1,0},{2,1},{3,2},{4,7},{5,4},{6,5},{7,6},{8,11},{9,8},{10,9... | collective-permute-start | bytes 2359304 | tf_op jit(solution)/shard_map/cond/branch_1_fun/ppermute | solution.py:262
  12.3 13.5 %collective-permute-done.7.refs_1_ = bf16[768,512]{1,0:T(8,128)(2,1)S(1)} collective-permute-done((bf16[768,512]{1,0:T(8,128)(2,1)S(1)}, bf16[768,512]{1,0:T(8,128)(2,1)S(1)}, u32[]{:S(2)}, u32[]{:S(2)}) %collective-permute-start.7) | collective-permute-done | bytes 786464 | tf_op jit(solution)/shard_map/cond/branch_1_fun/ppermute | solution.py:262
  25.8 3.4 %collective-permute-start.11 = (bf16[768,512]{1,0:T(8,128)(2,1)S(1)}, bf16[768,512]{1,0:T(8,128)(2,1)S(1)}, u32[]{:S(2)}, u32[]{:S(2)}) collective-permute-start(bf16[768,512]{1,0:T(8,128)(2,1)S(1)} %collective-permute-done.7.refs_1_), channel_id=1, source_target_pairs={{0,3},{1,0},{2,1},{3,2},{4,7},{5,4},{6,5},{7,6},{8,11},{9,8},{10,9... | collective-permute-start | bytes 2359304 | tf_op jit(solution)/shard_map/cond/branch_1_fun/ppermute | solution.py:262
  29.2 0.0 collective-permute-done.6.refs_0_
  29.2 0.0 collective-permute-start.10
  29.2 16.5 %collective-permute-done.8.refs_2_ = bf16[768,512]{1,0:T(8,128)(2,1)S(1)} collective-permute-done((bf16[768,512]{1,0:T(8,128)(2,1)S(1)}, bf16[768,512]{1,0:T(8,128)(2,1)S(1)}, u32[]{:S(2)}, u32[]{:S(2)}) %collective-permute-start.8) | collective-permute-done | bytes 786464 | tf_op jit(solution)/shard_map/cond/branch_1_fun/ppermute | solution.py:262
  45.7 0.0 collective-permute-done.9.refs_3_
  45.7 13.8 %collective-permute-done.11.refs_5_ = bf16[768,512]{1,0:T(8,128)(2,1)S(1)} collective-permute-done((bf16[768,512]{1,0:T(8,128)(2,1)S(1)}, bf16[768,512]{1,0:T(8,128)(2,1)S(1)}, u32[]{:S(2)}, u32[]{:S(2)}) %collective-permute-start.11) | collective-permute-done | bytes 786464 | tf_op jit(solution)/shard_map/cond/branch_1_fun/ppermute | solution.py:262
  59.5 3.1 %collective-permute-done.10.refs_4_ = bf16[768,512]{1,0:T(8,128)(2,1)S(1)} collective-permute-done((bf16[768,512]{1,0:T(8,128)(2,1)S(1)}, bf16[768,512]{1,0:T(8,128)(2,1)S(1)}, u32[]{:S(2)}, u32[]{:S(2)}) %collective-permute-start.10) | collective-permute-done | bytes 786464 | tf_op jit(solution)/shard_map/cond/branch_1_fun/ppermute | solution.py:262
  62.6 2.2 %branch_1_fun.1 = (bf16[4352,512]{1,0:T(8,128)(2,1)}, bf16[4352,512]{1,0:T(8,128)(2,1)}, bf16[4352,512]{1,0:T(8,128)(2,1)}) custom-call(bf16[768,512]{1,0:T(8,128)(2,1)S(1)} %collective-permute-done.6.refs_0_, bf16[768,512]{1,0:T(8,128)(2,1)S(1)} %collective-permute-done.7.refs_1_, bf16[768,512]{1,0:T(8,128)(2,1)S(1)} %collective-permute-done.8.refs_2_, ...), custom_call_target="tpu_custom_call" | custom-call | tf_op jit(solution)/shard_map/cond/branch_1_fun/pallas_call | solution.py:266
  65.2 21.7 %shard_map.74 = bf16[512,2176]{1,0:T(8,128)(2,1)} custom-call(s32[3]{0:T(128)} %get-tuple-element.22.facts, s32[5,16]{1,0:T(8,128)} %get-tuple-element.23.pairs, bf16[4352,512]{1,0:T(8,128)(2,1)} %get-tuple-element.24.x0, bf16[4352,512]{1,0:T(8,128)(2,1)} %get-tuple-element.26.x1, bf16[4352,512]{1,0:T(8,128)(2,1)} %get-tuple-element.27.x2, ...), custom_call_target="tpu_custom_call" | custom-call | tf_op jit(solution)/shard_map/pallas_call | solution.py:280
  86.9 47.8 %all_to_all.10 = bf16[32,16,2176]{2,1,0:T(8,128)(2,1)S(1)} all-to-all(bf16[32,16,2176]{2,1,0:T(8,128)(2,1)} %bitcast.13), channel_id=1, replica_groups=mesh['dp'=32,'mp'=4] {'dp'}, dimensions={0} | all-to-all | bytes 4456448 | tf_op jit(solution)/shard_map/all_to_all | solution.py:326
  134.7 2.2 %shard_map.75 = bf16[768,2048]{1,0:T(8,128)(2,1)S(1)} custom-call(bf16[512,2176]{1,0:T(8,128)(2,1)S(1)} %bitcast.12), custom_call_target="tpu_custom_call" | custom-call | tf_op jit(solution)/shard_map/pallas_call | solution.py:327
  136.9 43.2 %all_to_all.11 = bf16[32,24,2048]{2,1,0:T(8,128)(2,1)S(1)} all-to-all(bf16[32,24,2048]{2,1,0:T(8,128)(2,1)S(1)} %bitcast.11), channel_id=1, replica_groups=mesh['dp'=32,'mp'=4] {'dp'}, dimensions={0} | all-to-all | bytes 6291456 | tf_op jit(solution)/shard_map/all_to_all | solution.py:334
  180.1 3.2 %shard_map.76 = bf16[24,128,512]{2,1,0:T(8,128)(2,1)} custom-call(bf16[768,2048]{1,0:T(8,128)(2,1)S(1)} %bitcast.10), custom_call_target="tpu_custom_call" | custom-call | tf_op jit(solution)/shard_map/pallas_call | solution.py:335
Async XLA Ops:
  6.0 19.8 %collective-permute-start.7 = (bf16[768,512]{1,0:T(8,128)(2,1)S(1)}, bf16[768,512]{1,0:T(8,128)(2,1)S(1)}, u32[]{:S(2)}, u32[]{:S(2)}) collective-permute-start(bf16[768,512]{1,0:T(8,128)(2,1)S(1)} %get-tuple-element.31), channel_id=1, source_target_pairs={{0,3},{1,0},{2,1},{3,2},{4,7},{5,4},{6,5},{7,6},{8,11},{9,8},{10,9... | collective-permute-start | bytes 2359304 | tf_op jit(solution)/shard_map/cond/branch_1_fun/ppermute | solution.py:262
  9.6 19.6 %collective-permute-start.6 = (bf16[768,512]{1,0:T(8,128)(2,1)S(1)}, bf16[768,512]{1,0:T(8,128)(2,1)S(1)}, u32[]{:S(2)}, u32[]{:S(2)}) collective-permute-start(bf16[768,512]{1,0:T(8,128)(2,1)S(1)} %get-tuple-element.32), channel_id=1, source_target_pairs={{0,1},{1,2},{2,3},{3,0},{4,5},{5,6},{6,7},{7,4},{8,9},{9,10},{10,1... | collective-permute-start | bytes 2359304 | tf_op jit(solution)/shard_map/cond/branch_1_fun/ppermute | solution.py:262
  9.6 36.1 %collective-permute-start.8 = (bf16[768,512]{1,0:T(8,128)(2,1)S(1)}, bf16[768,512]{1,0:T(8,128)(2,1)S(1)}, u32[]{:S(2)}, u32[]{:S(2)}) collective-permute-start(bf16[768,512]{1,0:T(8,128)(2,1)S(1)} %get-tuple-element.31), channel_id=1, source_target_pairs={{0,1},{1,2},{2,3},{3,0},{4,5},{5,6},{6,7},{7,4},{8,9},{9,10},{10,1... | collective-permute-start | bytes 2359304 | tf_op jit(solution)/shard_map/cond/branch_1_fun/ppermute | solution.py:262
  9.7 36.1 %collective-permute-start.9 = (bf16[768,512]{1,0:T(8,128)(2,1)S(1)}, bf16[768,512]{1,0:T(8,128)(2,1)S(1)}, u32[]{:S(2)}, u32[]{:S(2)}) collective-permute-start(bf16[768,512]{1,0:T(8,128)(2,1)S(1)} %get-tuple-element.32), channel_id=1, source_target_pairs={{0,3},{1,0},{2,1},{3,2},{4,7},{5,4},{6,5},{7,6},{8,11},{9,8},{10,9... | collective-permute-start | bytes 2359304 | tf_op jit(solution)/shard_map/cond/branch_1_fun/ppermute | solution.py:262
  25.8 33.7 %collective-permute-start.11 = (bf16[768,512]{1,0:T(8,128)(2,1)S(1)}, bf16[768,512]{1,0:T(8,128)(2,1)S(1)}, u32[]{:S(2)}, u32[]{:S(2)}) collective-permute-start(bf16[768,512]{1,0:T(8,128)(2,1)S(1)} %collective-permute-done.7.refs_1_), channel_id=1, source_target_pairs={{0,3},{1,0},{2,1},{3,2},{4,7},{5,4},{6,5},{7,6},{8,11},{9,8},{10,9... | collective-permute-start | bytes 2359304 | tf_op jit(solution)/shard_map/cond/branch_1_fun/ppermute | solution.py:262
  29.2 33.4 %collective-permute-start.10 = (bf16[768,512]{1,0:T(8,128)(2,1)S(1)}, bf16[768,512]{1,0:T(8,128)(2,1)S(1)}, u32[]{:S(2)}, u32[]{:S(2)}) collective-permute-start(bf16[768,512]{1,0:T(8,128)(2,1)S(1)} %collective-permute-done.6.refs_0_), channel_id=1, source_target_pairs={{0,1},{1,2},{2,3},{3,0},{4,5},{5,6},{6,7},{7,4},{8,9},{9,10},{10,1... | collective-permute-start | bytes 2359304 | tf_op jit(solution)/shard_map/cond/branch_1_fun/ppermute | solution.py:262

commit v3 on v2

--- a/solution.py
+++ b/solution.py
@@ -137,9 +137,9 @@
 
     value_load = pltpu.make_async_copy(wv_in, wv, ready.at[0])
     query_load = pltpu.make_async_copy(wq_in, wq, ready.at[1])
-    begin(0, 0)
+    lax.fori_loop(0, tiles, begin, 0)
     value_load.start()
-    lax.fori_loop(1, chunks, begin, 0)
+    lax.fori_loop(tiles, chunks, begin, 0)
     query_load.start()
 
     def project(i, weight, out):
@@ -293,7 +293,7 @@
             pltpu.SemaphoreType.DMA((4, total // TILE)),
             pltpu.SemaphoreType.DMA((2,)),
         ],
-        compiler_params=pltpu.CompilerParams(vmem_limit_bytes=54 * 2**20),
+        compiler_params=pltpu.CompilerParams(vmem_limit_bytes=50 * 2**20),
     )(facts, pairs, x0, x1, x2, x3, wk, wv, wq)
 
 
@@ -319,7 +319,7 @@
             pltpu.SemaphoreType.DMA((2, bank)),
             pltpu.SemaphoreType.DMA((2 * bank + TILE // L,)),
         ],
-        compiler_params=pltpu.CompilerParams(vmem_limit_bytes=58 * 2**20),
+        compiler_params=pltpu.CompilerParams(vmem_limit_bytes=56 * 2**20),
     )(candidates.T, row_lengths.T, enc_bank.reshape(rows, width), dec_bank.reshape(rows, width))
     x1, x2, x3 = lax.switch(facts[0], [functools.partial(gather, size) for size in SIZES], packed)
     context = attend(facts, pairs, kept, x1, x2, x3, w_query, w_key, w_value)

time: 183 us -> 183 us (level)
  blocking collectives: 91.1 us -> 87 us
  waiting for transfers between devices: 46.8 us -> 50.2 us
    all_to_all x1, blocking collectives: 47.8 us -> 43.8 us  [on_device(): lax.all_to_all(context.reshape(shards, count, 4 * width + HD), 'dp', 0, 0...]
    ppermute x6, waiting for transfers between devices: 46.8 us -> 50.2 us  [gather(): lax.ppermute(x, 'mp', [(i, (i + step) % 4) for i in range(4)])]
where the time goes in v3:
time: 183 us; the launch traced here: 182 us
  blocking collectives  87 us (48%)
  waiting for transfers between devices  50.2 us (27%)
  Pallas kernels  33.4 us (18%)
  starting transfers between devices  9.76 us (5%)
    ppermute x6, waiting for transfers between devices, gather(): lax.ppermute(x, 'mp', [(i, (i + step) % 4) for i in range(4)])  50.2 us
    all_to_all x1, blocking collectives, on_device(): lax.all_to_all(context.reshape(shards, count, 4 * width + HD), 'dp', 0, 0...  43.8 us
    all_to_all x1, blocking collectives, on_device(): lax.all_to_all(routed.reshape(shards, GCAP, 4 * width), 'dp', 0, 0, tiled...  43.2 us
    pallas_call x1, Pallas kernels, attend(): pl.pallas_call(attend_kernel, out_shape=jax.ShapeDtypeStruct((n, 4 * widt...  20.5 us
    ppermute x6, starting transfers between devices, gather(): lax.ppermute(x, 'mp', [(i, (i + step) % 4) for i in range(4)])  9.76 us
    pallas_call x1, Pallas kernels, on_device(): pl.pallas_call(pack_kernel, out_shape=[jax.ShapeDtypeStruct((5, count), j...  5.19 us
  transfers between devices with their start and end apart: 6, of which 4 were waited for; matrix products, arithmetic and copies ran while one was open for 0% of the time, Pallas kernels for 0%

profile of v3, /device:TPU:1, one launch (start us, length us, event | category | flops | bytes accessed | tf_op | source)
XLA Modules:
  0.0 181.6 jit_solution(18231155903357242064)
XLA Ops:
  0.0 5.2 %shard_map.73 = (s32[5,16]{1,0:T(8,128)}, s32[3]{0:T(128)}, bf16[4352,512]{1,0:T(8,128)(2,1)S(1)}, bf16[4352,512]{1,0:T(8,128)(2,1)}) custom-call(s32[3,16]{1,0:T(4,128)} %bitcast.17, s32[2,16]{1,0:T(2,128)} %bitcast.18, bf16[2048,512]{1,0:T(8,128)(2,1)} %bitcast.15, bf16[2048,512]{1,0:T(8,128)(2,1)} %bitcast.16), custom_call_target="tpu_custom_call" | custom-call | tf_op jit(solution)/shard_map/pallas_call | solution.py:306
  5.8 0.0 copy-start
  5.8 0.0 copy-start.1
  5.8 0.0 copy-start.2
  5.8 62.9 %conditional.1 = ((bf16[4352,512]{1,0:T(8,128)(2,1)}, bf16[4352,512]{1,0:T(8,128)(2,1)}, bf16[4352,512]{1,0:T(8,128)(2,1)})) conditional(s32[]{:T(128)} %bitcast.4, bf16[4352,512]{1,0:T(8,128)(2,1)S(1)} %get-tuple-element.25, bf16[4352,512]{1,0:T(8,128)(2,1)S(1)} %get-tuple-element.25, ...), branch_computations={%region_0.0_spmd, %region_1.0_spmd, %region_2.0_spmd, %region_3.0_... | conditional | bytes 58720504 | solution.py:324
  5.8 0.1 fusion.2
  6.0 3.6 %collective-permute-start.13 = (bf16[832,512]{1,0:T(8,128)(2,1)S(1)}, bf16[832,512]{1,0:T(8,128)(2,1)S(1)}, u32[]{:S(2)}, u32[]{:S(2)}) collective-permute-start(bf16[832,512]{1,0:T(8,128)(2,1)S(1)} %get-tuple-element.33), channel_id=1, source_target_pairs={{0,3},{1,0},{2,1},{3,2},{4,7},{5,4},{6,5},{7,6},{8,11},{9,8},{10,9... | collective-permute-start | bytes 2555912 | tf_op jit(solution)/shard_map/cond/branch_2_fun/ppermute | solution.py:262
  9.6 0.0 collective-permute-start.12
  9.6 0.0 collective-permute-start.14
  9.6 2.7 %collective-permute-start.15 = (bf16[832,512]{1,0:T(8,128)(2,1)S(1)}, bf16[832,512]{1,0:T(8,128)(2,1)S(1)}, u32[]{:S(2)}, u32[]{:S(2)}) collective-permute-start(bf16[832,512]{1,0:T(8,128)(2,1)S(1)} %get-tuple-element.34), channel_id=1, source_target_pairs={{0,3},{1,0},{2,1},{3,2},{4,7},{5,4},{6,5},{7,6},{8,11},{9,8},{10,9... | collective-permute-start | bytes 2555912 | tf_op jit(solution)/shard_map/cond/branch_2_fun/ppermute | solution.py:262
  12.3 14.9 %collective-permute-done.13.refs_1_ = bf16[832,512]{1,0:T(8,128)(2,1)S(1)} collective-permute-done((bf16[832,512]{1,0:T(8,128)(2,1)S(1)}, bf16[832,512]{1,0:T(8,128)(2,1)S(1)}, u32[]{:S(2)}, u32[]{:S(2)}) %collective-permute-start.13) | collective-permute-done | bytes 852000 | tf_op jit(solution)/shard_map/cond/branch_2_fun/ppermute | solution.py:262
  27.2 3.4 %collective-permute-start.17 = (bf16[832,512]{1,0:T(8,128)(2,1)S(1)}, bf16[832,512]{1,0:T(8,128)(2,1)S(1)}, u32[]{:S(2)}, u32[]{:S(2)}) collective-permute-start(bf16[832,512]{1,0:T(8,128)(2,1)S(1)} %collective-permute-done.13.refs_1_), channel_id=1, source_target_pairs={{0,3},{1,0},{2,1},{3,2},{4,7},{5,4},{6,5},{7,6},{8,11},{9,8},{10,9... | collective-permute-start | bytes 2555912 | tf_op jit(solution)/shard_map/cond/branch_2_fun/ppermute | solution.py:262
  30.6 0.0 collective-permute-done.12.refs_0_
  30.6 0.0 collective-permute-start.16
  30.7 17.9 %collective-permute-done.14.refs_2_ = bf16[832,512]{1,0:T(8,128)(2,1)S(1)} collective-permute-done((bf16[832,512]{1,0:T(8,128)(2,1)S(1)}, bf16[832,512]{1,0:T(8,128)(2,1)S(1)}, u32[]{:S(2)}, u32[]{:S(2)}) %collective-permute-start.14) | collective-permute-done | bytes 852000 | tf_op jit(solution)/shard_map/cond/branch_2_fun/ppermute | solution.py:262
  48.6 0.0 collective-permute-done.15.refs_3_
  48.6 14.2 %collective-permute-done.17.refs_5_ = bf16[832,512]{1,0:T(8,128)(2,1)S(1)} collective-permute-done((bf16[832,512]{1,0:T(8,128)(2,1)S(1)}, bf16[832,512]{1,0:T(8,128)(2,1)S(1)}, u32[]{:S(2)}, u32[]{:S(2)}) %collective-permute-start.17) | collective-permute-done | bytes 852000 | tf_op jit(solution)/shard_map/cond/branch_2_fun/ppermute | solution.py:262
  62.8 3.1 %collective-permute-done.16.refs_4_ = bf16[832,512]{1,0:T(8,128)(2,1)S(1)} collective-permute-done((bf16[832,512]{1,0:T(8,128)(2,1)S(1)}, bf16[832,512]{1,0:T(8,128)(2,1)S(1)}, u32[]{:S(2)}, u32[]{:S(2)}) %collective-permute-start.16) | collective-permute-done | bytes 852000 | tf_op jit(solution)/shard_map/cond/branch_2_fun/ppermute | solution.py:262
  65.9 2.4 %branch_2_fun.1 = (bf16[4352,512]{1,0:T(8,128)(2,1)}, bf16[4352,512]{1,0:T(8,128)(2,1)}, bf16[4352,512]{1,0:T(8,128)(2,1)}) custom-call(bf16[832,512]{1,0:T(8,128)(2,1)S(1)} %collective-permute-done.12.refs_0_, bf16[832,512]{1,0:T(8,128)(2,1)S(1)} %collective-permute-done.13.refs_1_, bf16[832,512]{1,0:T(8,128)(2,1)S(1)} %collective-permute-done.14.refs_2_, ...), custom_call_target="tpu_custom_call" | custom-call | tf_op jit(solution)/shard_map/cond/branch_2_fun/pallas_call | solution.py:266
  68.7 0.0 copy-done
  68.7 0.0 copy-done.1
  68.7 0.0 copy-done.2
  68.7 20.5 %shard_map.74 = bf16[512,2176]{1,0:T(8,128)(2,1)} custom-call(s32[3]{0:T(128)S(1)} %copy-done.2, s32[5,16]{1,0:T(8,128)S(1)} %copy-done.1, bf16[4352,512]{1,0:T(8,128)(2,1)} %get-tuple-element.24.x0, bf16[4352,512]{1,0:T(8,128)(2,1)} %get-tuple-element.26.x1, bf16[4352,512]{1,0:T(8,128)(2,1)} %get-tuple-element.27.x2, ...), custom_call_target="tpu_custom_call" | custom-call | tf_op jit(solution)/shard_map/pallas_call | solution.py:280
  89.2 43.8 %all_to_all.10 = bf16[32,16,2176]{2,1,0:T(8,128)(2,1)S(1)} all-to-all(bf16[32,16,2176]{2,1,0:T(8,128)(2,1)} %bitcast.14), channel_id=1, replica_groups=mesh['dp'=32,'mp'=4] {'dp'}, dimensions={0} | all-to-all | bytes 4456448 | tf_op jit(solution)/shard_map/all_to_all | solution.py:326
  133.0 2.2 %shard_map.75 = bf16[768,2048]{1,0:T(8,128)(2,1)S(1)} custom-call(bf16[512,2176]{1,0:T(8,128)(2,1)S(1)} %bitcast.12), custom_call_target="tpu_custom_call" | custom-call | tf_op jit(solution)/shard_map/pallas_call | solution.py:327
  135.2 43.2 %all_to_all.11 = bf16[32,24,2048]{2,1,0:T(8,128)(2,1)S(1)} all-to-all(bf16[32,24,2048]{2,1,0:T(8,128)(2,1)S(1)} %bitcast.11), channel_id=1, replica_groups=mesh['dp'=32,'mp'=4] {'dp'}, dimensions={0} | all-to-all | bytes 6291456 | tf_op jit(solution)/shard_map/all_to_all | solution.py:334
  178.4 3.2 %shard_map.76 = bf16[24,128,512]{2,1,0:T(8,128)(2,1)} custom-call(bf16[768,2048]{1,0:T(8,128)(2,1)S(1)} %bitcast.10), custom_call_target="tpu_custom_call" | custom-call | tf_op jit(solution)/shard_map/pallas_call | solution.py:335
Async XLA Ops:
  5.8 62.9 %copy-start = (bf16[2048,512]{1,0:T(8,128)(2,1)S(1)}, bf16[2048,512]{1,0:T(8,128)(2,1)}, u32[]{:S(2)}) copy-start(bf16[2048,512]{1,0:T(8,128)(2,1)} %wk.1) | copy-start | bytes 6291460
  5.8 62.9 %copy-start.1 = (s32[5,16]{1,0:T(8,128)S(1)}, s32[5,16]{1,0:T(8,128)}, u32[]{:S(2)}) copy-start(s32[5,16]{1,0:T(8,128)} %get-tuple-element.23.pairs) | copy-start | bytes 964
  5.8 62.9 %copy-start.2 = (s32[3]{0:T(128)S(1)}, s32[3]{0:T(128)}, u32[]{:S(2)}) copy-start(s32[3]{0:T(128)} %get-tuple-element.22.facts) | copy-start | bytes 40
  6.0 21.3 %collective-permute-start.13 = (bf16[832,512]{1,0:T(8,128)(2,1)S(1)}, bf16[832,512]{1,0:T(8,128)(2,1)S(1)}, u32[]{:S(2)}, u32[]{:S(2)}) collective-permute-start(bf16[832,512]{1,0:T(8,128)(2,1)S(1)} %get-tuple-element.33), channel_id=1, source_target_pairs={{0,3},{1,0},{2,1},{3,2},{4,7},{5,4},{6,5},{7,6},{8,11},{9,8},{10,9... | collective-permute-start | bytes 2555912 | tf_op jit(solution)/shard_map/cond/branch_2_fun/ppermute | solution.py:262
  9.6 21.1 %collective-permute-start.12 = (bf16[832,512]{1,0:T(8,128)(2,1)S(1)}, bf16[832,512]{1,0:T(8,128)(2,1)S(1)}, u32[]{:S(2)}, u32[]{:S(2)}) collective-permute-start(bf16[832,512]{1,0:T(8,128)(2,1)S(1)} %get-tuple-element.34), channel_id=1, source_target_pairs={{0,1},{1,2},{2,3},{3,0},{4,5},{5,6},{6,7},{7,4},{8,9},{9,10},{10,1... | collective-permute-start | bytes 2555912 | tf_op jit(solution)/shard_map/cond/branch_2_fun/ppermute | solution.py:262
  9.6 39.0 %collective-permute-start.14 = (bf16[832,512]{1,0:T(8,128)(2,1)S(1)}, bf16[832,512]{1,0:T(8,128)(2,1)S(1)}, u32[]{:S(2)}, u32[]{:S(2)}) collective-permute-start(bf16[832,512]{1,0:T(8,128)(2,1)S(1)} %get-tuple-element.33), channel_id=1, source_target_pairs={{0,1},{1,2},{2,3},{3,0},{4,5},{5,6},{6,7},{7,4},{8,9},{9,10},{10,1... | collective-permute-start | bytes 2555912 | tf_op jit(solution)/shard_map/cond/branch_2_fun/ppermute | solution.py:262
  9.6 39.0 %collective-permute-start.15 = (bf16[832,512]{1,0:T(8,128)(2,1)S(1)}, bf16[832,512]{1,0:T(8,128)(2,1)S(1)}, u32[]{:S(2)}, u32[]{:S(2)}) collective-permute-start(bf16[832,512]{1,0:T(8,128)(2,1)S(1)} %get-tuple-element.34), channel_id=1, source_target_pairs={{0,3},{1,0},{2,1},{3,2},{4,7},{5,4},{6,5},{7,6},{8,11},{9,8},{10,9... | collective-permute-start | bytes 2555912 | tf_op jit(solution)/shard_map/cond/branch_2_fun/ppermute | solution.py:262
  27.2 35.5 %collective-permute-start.17 = (bf16[832,512]{1,0:T(8,128)(2,1)S(1)}, bf16[832,512]{1,0:T(8,128)(2,1)S(1)}, u32[]{:S(2)}, u32[]{:S(2)}) collective-permute-start(bf16[832,512]{1,0:T(8,128)(2,1)S(1)} %collective-permute-done.13.refs_1_), channel_id=1, source_target_pairs={{0,3},{1,0},{2,1},{3,2},{4,7},{5,4},{6,5},{7,6},{8,11},{9,8},{10,9... | collective-permute-start | bytes 2555912 | tf_op jit(solution)/shard_map/cond/branch_2_fun/ppermute | solution.py:262
  30.6 35.2 %collective-permute-start.16 = (bf16[832,512]{1,0:T(8,128)(2,1)S(1)}, bf16[832,512]{1,0:T(8,128)(2,1)S(1)}, u32[]{:S(2)}, u32[]{:S(2)}) collective-permute-start(bf16[832,512]{1,0:T(8,128)(2,1)S(1)} %collective-permute-done.12.refs_0_), channel_id=1, source_target_pairs={{0,1},{1,2},{2,3},{3,0},{4,5},{5,6},{6,7},{7,4},{8,9},{9,10},{10,1... | collective-permute-start | bytes 2555912 | tf_op jit(solution)/shard_map/cond/branch_2_fun/ppermute | solution.py:262

commit v4 on v3

--- a/solution.py
+++ b/solution.py
@@ -21,7 +21,7 @@
 HBM = pl.BlockSpec(memory_space=pltpu.HBM)
 
 
-def pack_kernel(cand, lens, enc, dec, out_pairs, facts, out, out_hbm, staged, starts, arrived, left):
+def pack_kernel(cand, lens, enc, dec, out_pairs, facts, out, staged, starts, arrived):
     rows = enc.shape[0] // L
     count = cand.shape[1]
     for row in range(rows):
@@ -59,11 +59,8 @@
             total = total + blocks
         facts[1 + column] = total * BLOCK
     bucket = jnp.int32(0)
-    size = jnp.int32(SIZES[0])
-    for low, high in zip(SIZES, SIZES[1:]):
-        over = total * BLOCK > low
-        bucket = bucket + over.astype(jnp.int32)
-        size = jnp.where(over, high, size)
+    for low in SIZES[:-1]:
+        bucket = bucket + (total * BLOCK > low).astype(jnp.int32)
     facts[0] = bucket
 
     def place(c, carry):
@@ -77,28 +74,12 @@
 
     lax.fori_loop(0, count, place, 0)
 
-    def leave(i):
-        rows = pl.ds(pl.multiple_of(i * L, L), L)
-        return pltpu.make_async_copy(out.at[rows], out_hbm.at[rows], left.at[i])
-
-    def begin_leave(i, carry):
-        leave(i).start()
-        return carry
-
-    def finish_leave(i, carry):
-        leave(i).wait()
-        return carry
-
-    pieces = (size + L - 1) // L
-    lax.fori_loop(0, pieces, begin_leave, 0)
-    lax.fori_loop(0, pieces, finish_leave, 0)
-
 
 def assemble_kernel(*refs):
-    pieces, (out1, out2, out3, done) = refs[:6], refs[6:]
+    pieces, (out0, out1, out2, out3, done) = refs[:8], refs[8:]
     half = pieces[0].shape[0]
     low, high = slice(0, half), slice(half, 2 * half)
-    outs = (out1.at[low], out3.at[high], out1.at[high], out3.at[low], out2.at[low], out2.at[high])
+    outs = (out1.at[low], out3.at[high], out1.at[high], out3.at[low], out2.at[low], out2.at[high], out0.at[low], out0.at[high])
     copies = [pltpu.make_async_copy(piece, out, done.at[k]) for k, (piece, out) in enumerate(zip(pieces, outs))]
     for copy in copies:
         copy.start()
@@ -262,14 +243,14 @@
     send = lambda x, step: lax.ppermute(x, "mp", [(i, (i + step) % 4) for i in range(4)])
     low, high = packed[:half], packed[half:size]
     left, right = send(low, 1), send(high, 3)
-    pieces = [left, right, send(high, 1), send(low, 3), send(left, 1), send(right, 3)]
+    pieces = [left, right, send(high, 1), send(low, 3), send(left, 1), send(right, 3), low, high]
     return pl.pallas_call(
         assemble_kernel,
-        out_shape=[jax.ShapeDtypeStruct(packed.shape, jnp.bfloat16)] * 3,
-        in_specs=[VMEM] * 6,
-        out_specs=[HBM] * 3,
-        scratch_shapes=[pltpu.SemaphoreType.DMA((6,))],
-        compiler_params=pltpu.CompilerParams(vmem_limit_bytes=13 * 2**20),
+        out_shape=[jax.ShapeDtypeStruct(packed.shape, jnp.bfloat16)] * 4,
+        in_specs=[VMEM] * 8,
+        out_specs=[HBM] * 4,
+        scratch_shapes=[pltpu.SemaphoreType.DMA((8,))],
+        compiler_params=pltpu.CompilerParams(vmem_limit_bytes=17 * 2**20),
     )(*pieces)
 
 
@@ -303,26 +284,24 @@
     bank = enc_bank.shape[0]
     width = enc_bank.shape[2]
     rows = bank * L
-    pairs, facts, packed, kept = pl.pallas_call(
+    pairs, facts, packed = pl.pallas_call(
         pack_kernel,
         out_shape=[
             jax.ShapeDtypeStruct((5, count), jnp.int32),
             jax.ShapeDtypeStruct((3,), jnp.int32),
             jax.ShapeDtypeStruct((2 * rows + TILE, width), jnp.bfloat16),
-            jax.ShapeDtypeStruct((2 * rows + TILE, width), jnp.bfloat16),
         ],
         in_specs=[SMEM, SMEM, HBM, HBM],
-        out_specs=[SMEM, SMEM, VMEM, HBM],
+        out_specs=[SMEM, SMEM, VMEM],
         scratch_shapes=[
             pltpu.VMEM((2, rows, width), jnp.bfloat16),
             pltpu.SMEM((2, bank), jnp.int32),
             pltpu.SemaphoreType.DMA((2, bank)),
-            pltpu.SemaphoreType.DMA((2 * bank + TILE // L,)),
         ],
         compiler_params=pltpu.CompilerParams(vmem_limit_bytes=56 * 2**20),
     )(candidates.T, row_lengths.T, enc_bank.reshape(rows, width), dec_bank.reshape(rows, width))
-    x1, x2, x3 = lax.switch(facts[0], [functools.partial(gather, size) for size in SIZES], packed)
-    context = attend(facts, pairs, kept, x1, x2, x3, w_query, w_key, w_value)
+    x0, x1, x2, x3 = lax.switch(facts[0], [functools.partial(gather, size) for size in SIZES], packed)
+    context = attend(facts, pairs, x0, x1, x2, x3, w_query, w_key, w_value)
     spread = lax.all_to_all(context.reshape(shards, count, 4 * width + HD), "dp", 0, 0, tiled=True)
     routed = pl.pallas_call(
         route_kernel,

time: 183 us -> 183 us (level); the launches traced: 182 us -> 185 us
  blocking collectives: 87 us -> 97.3 us
  waiting for transfers between devices: 50.2 us -> 45.9 us
  Pallas kernels: 33.4 us -> 30.9 us
    all_to_all x1, blocking collectives: 43.8 us -> 54 us  [on_device(): lax.all_to_all(context.reshape(shards, count, 4 * width + HD), 'dp', 0, 0...]
    ppermute x6, waiting for transfers between devices: 50.2 us -> 45.9 us  [gather(): lax.ppermute(x, 'mp', [(i, (i + step) % 4) for i in range(4)])]
where the time goes in v4:
time: 183 us; the launch traced here: 185 us
  blocking collectives  97.3 us (53%)
  waiting for transfers between devices  45.9 us (25%)
  Pallas kernels  30.9 us (17%)
  starting transfers between devices  9.76 us (5%)
    all_to_all x1, blocking collectives, on_device(): lax.all_to_all(context.reshape(shards, count, 4 * width + HD), 'dp', 0, 0...  54 us
    ppermute x6, waiting for transfers between devices, gather(): lax.ppermute(x, 'mp', [(i, (i + step) % 4) for i in range(4)])  45.9 us
    all_to_all x1, blocking collectives, on_device(): lax.all_to_all(routed.reshape(shards, GCAP, 4 * width), 'dp', 0, 0, tiled...  43.2 us
    pallas_call x1, Pallas kernels, attend(): pl.pallas_call(attend_kernel, out_shape=jax.ShapeDtypeStruct((n, 4 * widt...  19.1 us
    ppermute x6, starting transfers between devices, gather(): lax.ppermute(x, 'mp', [(i, (i + step) % 4) for i in range(4)])  9.76 us
    pallas_call x1, Pallas kernels, on_device(): pl.pallas_call(pack_kernel, out_shape=[jax.ShapeDtypeStruct((5, count), j...  3.71 us
  transfers between devices with their start and end apart: 6, of which 4 were waited for; matrix products, arithmetic and copies ran while one was open for 0% of the time, Pallas kernels for 0%

profile of v4, /device:TPU:1, one launch (start us, length us, event | category | flops | bytes accessed | tf_op | source)
XLA Modules:
  0.0 185.1 jit_solution(16984711460922460044)
XLA Ops:
  0.0 3.7 %shard_map.73 = (s32[5,16]{1,0:T(8,128)}, s32[3]{0:T(128)}, bf16[4352,512]{1,0:T(8,128)(2,1)S(1)}) custom-call(s32[3,16]{1,0:T(4,128)} %bitcast.17, s32[2,16]{1,0:T(2,128)} %bitcast.18, bf16[2048,512]{1,0:T(8,128)(2,1)} %bitcast.15, bf16[2048,512]{1,0:T(8,128)(2,1)} %bitcast.16), custom_call_target="tpu_custom_call" | custom-call | tf_op jit(solution)/shard_map/pallas_call | solution.py:287
  4.3 0.0 copy-start
  4.3 0.0 copy-start.1
  4.3 0.0 copy-start.2
  4.3 58.9 %conditional.1 = ((bf16[4352,512]{1,0:T(8,128)(2,1)}, bf16[4352,512]{1,0:T(8,128)(2,1)}, bf16[4352,512]{1,0:T(8,128)(2,1)}, bf16[4352,512]{1,0:T(8,128)(2,1)})) conditional(s32[]{:T(128)} %bitcast.4, bf16[4352,512]{1,0:T(8,128)(2,1)S(1)} %get-tuple-element.24, bf16[4352,512]{1,0:T(8,128)(2,1)S(1)} %get-tuple-element.24, ...), branch_computations={%region_0.0_spmd, %region_1.0_spmd, %region_2.0_spmd, %region_3.0_... | conditional | bytes 58720504 | solution.py:303
  4.4 0.1 fusion.1
  4.5 3.6 %collective-permute-start.7 = (bf16[768,512]{1,0:T(8,128)(2,1)S(1)}, bf16[768,512]{1,0:T(8,128)(2,1)S(1)}, u32[]{:S(2)}, u32[]{:S(2)}) collective-permute-start(bf16[768,512]{1,0:T(8,128)(2,1)S(1)} %get-tuple-element.31.refs_7_), channel_id=1, source_target_pairs={{0,3},{1,0},{2,1},{3,2},{4,7},{5,4},{6,5},{7,6},{8,11},{9,8},{10,9... | collective-permute-start | bytes 2359304 | tf_op jit(solution)/shard_map/cond/branch_1_fun/ppermute | solution.py:243
  8.1 0.0 collective-permute-start.6
  8.1 0.0 collective-permute-start.8
  8.1 2.7 %collective-permute-start.9 = (bf16[768,512]{1,0:T(8,128)(2,1)S(1)}, bf16[768,512]{1,0:T(8,128)(2,1)S(1)}, u32[]{:S(2)}, u32[]{:S(2)}) collective-permute-start(bf16[768,512]{1,0:T(8,128)(2,1)S(1)} %get-tuple-element.32.refs_6_), channel_id=1, source_target_pairs={{0,3},{1,0},{2,1},{3,2},{4,7},{5,4},{6,5},{7,6},{8,11},{9,8},{10,9... | collective-permute-start | bytes 2359304 | tf_op jit(solution)/shard_map/cond/branch_1_fun/ppermute | solution.py:243
  10.8 13.6 %collective-permute-done.7.refs_1_ = bf16[768,512]{1,0:T(8,128)(2,1)S(1)} collective-permute-done((bf16[768,512]{1,0:T(8,128)(2,1)S(1)}, bf16[768,512]{1,0:T(8,128)(2,1)S(1)}, u32[]{:S(2)}, u32[]{:S(2)}) %collective-permute-start.7) | collective-permute-done | bytes 786464 | tf_op jit(solution)/shard_map/cond/branch_1_fun/ppermute | solution.py:243
  24.4 3.4 %collective-permute-start.11 = (bf16[768,512]{1,0:T(8,128)(2,1)S(1)}, bf16[768,512]{1,0:T(8,128)(2,1)S(1)}, u32[]{:S(2)}, u32[]{:S(2)}) collective-permute-start(bf16[768,512]{1,0:T(8,128)(2,1)S(1)} %collective-permute-done.7.refs_1_), channel_id=1, source_target_pairs={{0,3},{1,0},{2,1},{3,2},{4,7},{5,4},{6,5},{7,6},{8,11},{9,8},{10,9... | collective-permute-start | bytes 2359304 | tf_op jit(solution)/shard_map/cond/branch_1_fun/ppermute | solution.py:243
  27.8 0.0 collective-permute-done.6.refs_0_
  27.8 0.0 collective-permute-start.10
  27.8 16.5 %collective-permute-done.8.refs_2_ = bf16[768,512]{1,0:T(8,128)(2,1)S(1)} collective-permute-done((bf16[768,512]{1,0:T(8,128)(2,1)S(1)}, bf16[768,512]{1,0:T(8,128)(2,1)S(1)}, u32[]{:S(2)}, u32[]{:S(2)}) %collective-permute-start.8) | collective-permute-done | bytes 786464 | tf_op jit(solution)/shard_map/cond/branch_1_fun/ppermute | solution.py:243
  44.4 0.0 collective-permute-done.9.refs_3_
  44.4 12.7 %collective-permute-done.11.refs_5_ = bf16[768,512]{1,0:T(8,128)(2,1)S(1)} collective-permute-done((bf16[768,512]{1,0:T(8,128)(2,1)S(1)}, bf16[768,512]{1,0:T(8,128)(2,1)S(1)}, u32[]{:S(2)}, u32[]{:S(2)}) %collective-permute-start.11) | collective-permute-done | bytes 786464 | tf_op jit(solution)/shard_map/cond/branch_1_fun/ppermute | solution.py:243
  57.1 3.1 %collective-permute-done.10.refs_4_ = bf16[768,512]{1,0:T(8,128)(2,1)S(1)} collective-permute-done((bf16[768,512]{1,0:T(8,128)(2,1)S(1)}, bf16[768,512]{1,0:T(8,128)(2,1)S(1)}, u32[]{:S(2)}, u32[]{:S(2)}) %collective-permute-start.10) | collective-permute-done | bytes 786464 | tf_op jit(solution)/shard_map/cond/branch_1_fun/ppermute | solution.py:243
  60.2 2.7 %branch_1_fun.1 = (bf16[4352,512]{1,0:T(8,128)(2,1)}, bf16[4352,512]{1,0:T(8,128)(2,1)}, bf16[4352,512]{1,0:T(8,128)(2,1)}, bf16[4352,512]{1,0:T(8,128)(2,1)}) custom-call(bf16[768,512]{1,0:T(8,128)(2,1)S(1)} %collective-permute-done.6.refs_0_, bf16[768,512]{1,0:T(8,128)(2,1)S(1)} %collective-permute-done.7.refs_1_, ...), custom_call_target="tpu_custom_call" | custom-call | tf_op jit(solution)/shard_map/cond/branch_1_fun/pallas_call | solution.py:247
  63.3 0.0 copy-done
  63.3 0.0 copy-done.1
  63.3 0.0 copy-done.2
  63.3 19.1 %shard_map.74 = bf16[512,2176]{1,0:T(8,128)(2,1)} custom-call(s32[3]{0:T(128)S(1)} %copy-done.2, s32[5,16]{1,0:T(8,128)S(1)} %copy-done.1, bf16[4352,512]{1,0:T(8,128)(2,1)} %get-tuple-element.25.x0, bf16[4352,512]{1,0:T(8,128)(2,1)} %get-tuple-element.26.x1, bf16[4352,512]{1,0:T(8,128)(2,1)} %get-tuple-element.27.x2, ...), custom_call_target="tpu_custom_call" | custom-call | tf_op jit(solution)/shard_map/pallas_call | solution.py:261
  82.4 54.0 %all_to_all.10 = bf16[32,16,2176]{2,1,0:T(8,128)(2,1)S(1)} all-to-all(bf16[32,16,2176]{2,1,0:T(8,128)(2,1)} %bitcast.14), channel_id=1, replica_groups=mesh['dp'=32,'mp'=4] {'dp'}, dimensions={0} | all-to-all | bytes 4456448 | tf_op jit(solution)/shard_map/all_to_all | solution.py:305
  136.5 2.2 %shard_map.75 = bf16[768,2048]{1,0:T(8,128)(2,1)S(1)} custom-call(bf16[512,2176]{1,0:T(8,128)(2,1)S(1)} %bitcast.12), custom_call_target="tpu_custom_call" | custom-call | tf_op jit(solution)/shard_map/pallas_call | solution.py:306
  138.7 43.2 %all_to_all.11 = bf16[32,24,2048]{2,1,0:T(8,128)(2,1)S(1)} all-to-all(bf16[32,24,2048]{2,1,0:T(8,128)(2,1)S(1)} %bitcast.11), channel_id=1, replica_groups=mesh['dp'=32,'mp'=4] {'dp'}, dimensions={0} | all-to-all | bytes 6291456 | tf_op jit(solution)/shard_map/all_to_all | solution.py:313
  181.9 3.2 %shard_map.76 = bf16[24,128,512]{2,1,0:T(8,128)(2,1)} custom-call(bf16[768,2048]{1,0:T(8,128)(2,1)S(1)} %bitcast.10), custom_call_target="tpu_custom_call" | custom-call | tf_op jit(solution)/shard_map/pallas_call | solution.py:314
Async XLA Ops:
  4.3 59.0 %copy-start = (bf16[2048,512]{1,0:T(8,128)(2,1)S(1)}, bf16[2048,512]{1,0:T(8,128)(2,1)}, u32[]{:S(2)}) copy-start(bf16[2048,512]{1,0:T(8,128)(2,1)} %wk.1) | copy-start | bytes 6291460
  4.3 59.0 %copy-start.1 = (s32[5,16]{1,0:T(8,128)S(1)}, s32[5,16]{1,0:T(8,128)}, u32[]{:S(2)}) copy-start(s32[5,16]{1,0:T(8,128)} %get-tuple-element.23.pairs) | copy-start | bytes 964
  4.3 59.0 %copy-start.2 = (s32[3]{0:T(128)S(1)}, s32[3]{0:T(128)}, u32[]{:S(2)}) copy-start(s32[3]{0:T(128)} %get-tuple-element.22.facts) | copy-start | bytes 40
  4.5 19.9 %collective-permute-start.7 = (bf16[768,512]{1,0:T(8,128)(2,1)S(1)}, bf16[768,512]{1,0:T(8,128)(2,1)S(1)}, u32[]{:S(2)}, u32[]{:S(2)}) collective-permute-start(bf16[768,512]{1,0:T(8,128)(2,1)S(1)} %get-tuple-element.31.refs_7_), channel_id=1, source_target_pairs={{0,3},{1,0},{2,1},{3,2},{4,7},{5,4},{6,5},{7,6},{8,11},{9,8},{10,9... | collective-permute-start | bytes 2359304 | tf_op jit(solution)/shard_map/cond/branch_1_fun/ppermute | solution.py:243
  8.1 19.7 %collective-permute-start.6 = (bf16[768,512]{1,0:T(8,128)(2,1)S(1)}, bf16[768,512]{1,0:T(8,128)(2,1)S(1)}, u32[]{:S(2)}, u32[]{:S(2)}) collective-permute-start(bf16[768,512]{1,0:T(8,128)(2,1)S(1)} %get-tuple-element.32.refs_6_), channel_id=1, source_target_pairs={{0,1},{1,2},{2,3},{3,0},{4,5},{5,6},{6,7},{7,4},{8,9},{9,10},{10,1... | collective-permute-start | bytes 2359304 | tf_op jit(solution)/shard_map/cond/branch_1_fun/ppermute | solution.py:243
  8.1 36.3 %collective-permute-start.8 = (bf16[768,512]{1,0:T(8,128)(2,1)S(1)}, bf16[768,512]{1,0:T(8,128)(2,1)S(1)}, u32[]{:S(2)}, u32[]{:S(2)}) collective-permute-start(bf16[768,512]{1,0:T(8,128)(2,1)S(1)} %get-tuple-element.31.refs_7_), channel_id=1, source_target_pairs={{0,1},{1,2},{2,3},{3,0},{4,5},{5,6},{6,7},{7,4},{8,9},{9,10},{10,1... | collective-permute-start | bytes 2359304 | tf_op jit(solution)/shard_map/cond/branch_1_fun/ppermute | solution.py:243
  8.1 36.2 %collective-permute-start.9 = (bf16[768,512]{1,0:T(8,128)(2,1)S(1)}, bf16[768,512]{1,0:T(8,128)(2,1)S(1)}, u32[]{:S(2)}, u32[]{:S(2)}) collective-permute-start(bf16[768,512]{1,0:T(8,128)(2,1)S(1)} %get-tuple-element.32.refs_6_), channel_id=1, source_target_pairs={{0,3},{1,0},{2,1},{3,2},{4,7},{5,4},{6,5},{7,6},{8,11},{9,8},{10,9... | collective-permute-start | bytes 2359304 | tf_op jit(solution)/shard_map/cond/branch_1_fun/ppermute | solution.py:243
  24.4 32.7 %collective-permute-start.11 = (bf16[768,512]{1,0:T(8,128)(2,1)S(1)}, bf16[768,512]{1,0:T(8,128)(2,1)S(1)}, u32[]{:S(2)}, u32[]{:S(2)}) collective-permute-start(bf16[768,512]{1,0:T(8,128)(2,1)S(1)} %collective-permute-done.7.refs_1_), channel_id=1, source_target_pairs={{0,3},{1,0},{2,1},{3,2},{4,7},{5,4},{6,5},{7,6},{8,11},{9,8},{10,9... | collective-permute-start | bytes 2359304 | tf_op jit(solution)/shard_map/cond/branch_1_fun/ppermute | solution.py:243
  27.8 32.4 %collective-permute-start.10 = (bf16[768,512]{1,0:T(8,128)(2,1)S(1)}, bf16[768,512]{1,0:T(8,128)(2,1)S(1)}, u32[]{:S(2)}, u32[]{:S(2)}) collective-permute-start(bf16[768,512]{1,0:T(8,128)(2,1)S(1)} %collective-permute-done.6.refs_0_), channel_id=1, source_target_pairs={{0,1},{1,2},{2,3},{3,0},{4,5},{5,6},{6,7},{7,4},{8,9},{9,10},{10,1... | collective-permute-start | bytes 2359304 | tf_op jit(solution)/shard_map/cond/branch_1_fun/ppermute | solution.py:243
